TPU v7x, 32 devices: a whole 2x2x4 slice. The times are simulated.
32 devices in a mesh: groups: 2 (over y), expert: 8 (over z, core), dp: 2 (over x).
Axes of the slice: x: 2, y: 2, z: 4, core: 2. Of those that a mesh axis runs over, the one named last changes fastest.
Arguments:
- tokens: bfloat16 [4096, 2048], P(('groups', 'expert', 'dp')), parts along dimension 0, may hold values from -6 to 6
- out_grads: bfloat16 [4096, 2048], P(('groups', 'expert', 'dp')), parts along dimension 0, may hold values from -3 to 3
- routes: int32 [4096, 8], P(('groups', 'expert', 'dp')), parts along dimension 0, may hold values from 0 to 15, all different within a row; in each aligned block of 128 rows (0 to 127, 128 to 255, ...) at most 72 rows name the same one
- gates: bfloat16 [4096, 8], P(('groups', 'expert', 'dp')), parts along dimension 0, may hold values from 0.049804688 to 0.5
- gate_weight: bfloat16 [16, 2048, 384], P('expert'), may hold values from -0.125 to 0.125
- up_weight: bfloat16 [16, 2048, 384], P('expert'), may hold values from -0.125 to 0.125
- down_weight: bfloat16 [16, 384, 2048], P('expert'), may hold values from -0.3125 to 0.3125
Outputs:
- input_grads: bfloat16 [4096, 2048], P(('groups', 'expert', 'dp')), parts along dimension 0
- gate_grads: bfloat16 [4096, 8], P(('groups', 'expert', 'dp')), parts along dimension 0
- gate_weight_grads: bfloat16 [32, 2048, 384], P(('groups', 'expert'), 'dp'), parts along dimension 0
- up_weight_grads: bfloat16 [32, 2048, 384], P(('groups', 'expert'), 'dp'), parts along dimension 0
- down_weight_grads: bfloat16 [32, 384, 2048], P(('groups', 'expert'), None, 'dp'), parts along dimension 0
There are 2 independent parts, one for each index of `groups`. A program takes and returns all parts, laid end to end along the dimension named above; an argument that names none is the same for every part. Nothing has to cross between parts.
Inputs may be any that keep to these rules, and one draw needn't show every extreme that they name: `routes`: each row names 8 different experts; among the rows of one device no expert is named more than 72 times, and in every draw some expert is named exactly 72 times by the rows of some device.
All inputs are finite; a program needn't handle non-finite values.
Results may differ from a plain program's by a relative error of at most 0.012.
Values may be sent and summed in bfloat16 or wider, within the bound.
A program may use at most 128 MiB of HBM per device.

v0:
```python
import jax
import jax.numpy as jnp
from jax import lax
from jax.sharding import PartitionSpec as P


def project_in(rows_x, gate_weight, up_weight):
    pre_gate = jnp.einsum("slcd,ldf->slcf", rows_x, gate_weight, preferred_element_type=jnp.float32)
    pre_up = jnp.einsum("slcd,ldf->slcf", rows_x, up_weight, preferred_element_type=jnp.float32)
    return (pre_gate, pre_up)


def per_device(tokens, out_grads, routes, gates, gate_weight, up_weight, down_weight):
    tok_rows, feature_width = tokens.shape
    top_count = routes.shape[1]
    local_experts = gate_weight.shape[0]
    group_count = lax.axis_size("expert")
    expert_count = local_experts * group_count
    capacity = min(
        tok_rows, max(2, (tok_rows * top_count * 9 + expert_count * 8 - 1) // (expert_count * 8))
    )
    flat_routes = routes.reshape(-1)
    onehot = (flat_routes[:, None] == jnp.arange(expert_count, dtype=jnp.int32)[None, :]).astype(
        jnp.int32
    )
    positions = jnp.sum((jnp.cumsum(onehot, axis=0) - 1) * onehot, axis=1)
    slot_index = flat_routes * capacity + positions
    sentinel = tok_rows * top_count
    slot_table = (
        jnp.full((expert_count * capacity,), sentinel, jnp.int32)
        .at[slot_index]
        .set(jnp.arange(sentinel, dtype=jnp.int32))
    )
    owners = slot_table // top_count
    padded_x = jnp.concatenate([tokens, jnp.zeros((1, feature_width), tokens.dtype)], axis=0)
    padded_dy = jnp.concatenate([out_grads, jnp.zeros((1, feature_width), out_grads.dtype)], axis=0)
    padded_gate = jnp.concatenate([gates.reshape(-1), jnp.zeros((1,), gates.dtype)], axis=0)
    shape_rows = (group_count, local_experts * capacity, feature_width)
    block_shape = (group_count, local_experts, capacity, feature_width)
    send_x = jnp.take(padded_x, owners, axis=0).reshape(shape_rows)
    send_dy = jnp.take(padded_dy, owners, axis=0).reshape(shape_rows)
    send_gate = jnp.take(padded_gate, slot_table).reshape(group_count, local_experts * capacity)
    recv_x, recv_dy, recv_gate = (
        lax.all_to_all(send_x, "expert", split_axis=0, concat_axis=0, tiled=True),
        lax.all_to_all(send_dy, "expert", split_axis=0, concat_axis=0, tiled=True),
        lax.all_to_all(send_gate, "expert", split_axis=0, concat_axis=0, tiled=True),
    )
    pre_gate, pre_up = project_in(recv_x.reshape(block_shape), gate_weight, up_weight)
    rows_x = recv_x.reshape(block_shape)
    rows_dy = recv_dy.reshape(block_shape)
    gate_col = recv_gate.reshape(group_count, local_experts, capacity, 1).astype(jnp.float32)
    sigmoid_gate = jax.nn.sigmoid(pre_gate)
    activated = pre_gate * sigmoid_gate
    hidden = activated * pre_up
    gated_hidden = (gate_col * hidden).astype(jnp.bfloat16)
    back_raw = jnp.einsum(
        "slcd,lfd->slcf", rows_dy, down_weight, preferred_element_type=jnp.float32
    )
    route_grad = jnp.sum(hidden * back_raw, axis=-1).astype(jnp.bfloat16)
    back = gate_col * back_raw
    grad_gate = (back * pre_up * sigmoid_gate * (1.0 + pre_gate * (1.0 - sigmoid_gate))).astype(
        jnp.bfloat16
    )
    grad_up = (back * activated).astype(jnp.bfloat16)
    down_part = jnp.einsum(
        "slcf,slcd->lfd", gated_hidden, rows_dy, preferred_element_type=jnp.float32
    ).astype(jnp.bfloat16)
    row_grads = (
        jnp.einsum("slcf,ldf->slcd", grad_gate, gate_weight, preferred_element_type=jnp.float32)
        + jnp.einsum("slcf,ldf->slcd", grad_up, up_weight, preferred_element_type=jnp.float32)
    ).astype(jnp.bfloat16)
    back_rows, back_route = (
        lax.all_to_all(
            row_grads.reshape(shape_rows), "expert", split_axis=0, concat_axis=0, tiled=True
        ),
        lax.all_to_all(
            route_grad.reshape(group_count, local_experts * capacity),
            "expert",
            split_axis=0,
            concat_axis=0,
            tiled=True,
        ),
    )
    picked = jnp.take(back_rows.reshape(expert_count * capacity, feature_width), slot_index, axis=0)
    picked = picked.reshape(tok_rows, top_count, feature_width)
    input_grads = jnp.sum(picked, axis=1, dtype=jnp.float32).astype(jnp.bfloat16)
    gate_grads = jnp.take(back_route.reshape(-1), slot_index).reshape(tok_rows, top_count)
    gate_part = jnp.einsum(
        "slcd,slcf->ldf", rows_x, grad_gate, preferred_element_type=jnp.float32
    ).astype(jnp.bfloat16)
    up_part = jnp.einsum(
        "slcd,slcf->ldf", rows_x, grad_up, preferred_element_type=jnp.float32
    ).astype(jnp.bfloat16)
    gate_sum, up_sum, down_sum = (
        lax.psum_scatter(gate_part, "dp", scatter_dimension=1, tiled=True).astype(jnp.float32),
        lax.psum_scatter(up_part, "dp", scatter_dimension=1, tiled=True).astype(jnp.float32),
        lax.psum_scatter(down_part, "dp", scatter_dimension=2, tiled=True).astype(jnp.float32),
    )
    return (
        input_grads,
        gate_grads,
        gate_sum.astype(jnp.bfloat16),
        up_sum.astype(jnp.bfloat16),
        down_sum.astype(jnp.bfloat16),
    )


def solution(mesh):
    in_specs = (
        P(("groups", "expert", "dp"), None),
        P(("groups", "expert", "dp"), None),
        P(("groups", "expert", "dp"), None),
        P(("groups", "expert", "dp"), None),
        P("expert", None, None),
        P("expert", None, None),
        P("expert", None, None),
    )
    out_specs = (
        P(("groups", "expert", "dp"), None),
        P(("groups", "expert", "dp"), None),
        P(("groups", "expert"), "dp", None),
        P(("groups", "expert"), "dp", None),
        P(("groups", "expert"), None, "dp"),
    )
    return jax.shard_map(
        per_device, mesh=mesh, in_specs=in_specs, out_specs=out_specs, check_vma=False
    )
```

profile of v0, /device:TPU:0, one launch (start us, length us, event | category | flops | bytes accessed | tf_op | source)
XLA Modules:
  0.0 462.9 jit_solution(1576886883880407843)
XLA Ops:
  7.2 0.9 copy.46
  8.3 0.8 copy.51
  9.2 4.5 reduce-window.6
  14.3 4.3 scatter_custom_fusion
  18.7 7.3 %gather_fusion = bf16[1152]{0:T(1024)(128)(2,1)S(1)} fusion(bf16[1025]{0:T(1024)(128)(2,1)S(1)} %pad_maximum_fusion, s32[2048]{0:T(1024)S(1)} %pad_clamp_fusion.1), kind=kCustom, calls=%fused_computation.2 | custom fusion | bytes 9216 | tf_op jit(solution)/shard_map/jit(_take)/gather | solution.py:42
  26.0 0.7 select_n.75
  26.7 6.3 %all-to-all-start = ((bf16[8,1,144]{2,1,0:T(2,128)(2,1)}), bf16[8,1,144]{2,1,0:T(2,128)(2,1)S(1)}, u32[]{:S(2)}, u32[]{:S(2)}) async-start(bf16[8,1,144]{2,1,0:T(2,128)(2,1)} %select_n.75), calls=%async_computation | async-start | bytes 16384 | tf_op jit(solution)/shard_map/all_to_all | solution.py:46
  33.0 1.9 concatenate.11
  34.9 1.9 concatenate.10
  36.8 11.9 %gather_fusion.3 = bf16[1152,2048]{1,0:T(8,128)(2,1)} fusion(bf16[129,2048]{1,0:T(8,128)(2,1)} %concatenate.10, s32[2048]{0:T(1024)S(1)} %pad_clamp_fusion), kind=kCustom, calls=%fused_computation.clone | custom fusion | bytes 9441792 | tf_op jit(solution)/shard_map/jit(_take)/gather | solution.py:41
  48.7 11.8 %gather_fusion.4 = bf16[1152,2048]{1,0:T(8,128)(2,1)} fusion(bf16[129,2048]{1,0:T(8,128)(2,1)} %concatenate.11, s32[2048]{0:T(1024)S(1)} %pad_clamp_fusion), kind=kCustom, calls=%fused_computation.1.clone | custom fusion | bytes 9441792 | tf_op jit(solution)/shard_map/jit(_take)/gather | solution.py:40
  60.5 8.7 %broadcast_select_fusion.1 = (bf16[1152,2048]{1,0:T(8,128)(2,1)}, bf16[1152,2048]{1,0:T(8,128)(2,1)}) fusion(bf16[1152,2048]{1,0:T(8,128)(2,1)} %gather_fusion.3, pred[1152]{0:T(1024)(128)(4,1)S(1)} %get-tuple-element.23, bf16[1152,2048]{1,0:T(8,128)(2,1)} %gather_fusion.4), kind=kLoop, calls=%fused_computation.12 | loop fusion | flops 4718592 | bytes 18875520 | tf_op jit(solution)/shard_map/jit(_take)/select_n | solution.py:41
  69.1 110.5 %all_to_all.27 = bf16[8,144,2048]{2,1,0:T(8,128)(2,1)} all-to-all(bf16[8,144,2048]{2,1,0:T(8,128)(2,1)} %bitcast.110), channel_id=1, replica_groups=mesh['groups'=2,'expert'=8,'dp'=2] {'expert'}, dimensions={0} | all-to-all | bytes 9437184 | tf_op jit(solution)/shard_map/all_to_all | solution.py:44
  179.7 4.6 all-to-all-start.1
  184.6 6.3 %fusion.2 = f32[2,8,72,384]{3,2,1,0:T(8,128)} fusion(bf16[8,2,72,2048]{3,2,1,0:T(8,128)(2,1)} %bitcast.112, bf16[2,2048,384]{2,1,0:T(8,128)(2,1)S(1)} %copy-done), kind=kOutput, calls=%fused_computation.15 | convolution fusion | flops 1811939328 | bytes 9633792 | tf_op jit(solution)/shard_map/slcd,ldf->slcf/dot_general | solution.py:8
  190.9 3.8 fusion.4
  194.8 94.7 %all-to-all-done.1 = bf16[8,144,2048]{2,1,0:T(8,128)(2,1)} async-done(((bf16[8,144,2048]{2,1,0:T(8,128)(2,1)}), bf16[8,144,2048]{2,1,0:T(8,128)(2,1)}, u32[]{:S(2)}, u32[]{:S(2)}) %all-to-all-start.1) | async-done | bytes 4718624 | tf_op jit(solution)/shard_map/all_to_all | solution.py:45
  289.5 7.9 %bitcast_convert_fusion = bf16[2,384,2048]{2,1,0:T(8,128)(2,1)} fusion(bf16[8,2,72,2048]{3,2,1,0:T(8,128)(2,1)} %bitcast.5, f32[8,2,72]{2,0,1:T(8,128)S(1)} %copy.53, f32[2,8,72,384]{3,2,1,0:T(8,128)} %fusion.4, f32[2,8,72,384]{3,2,1,0:T(8,128)} %fusion.2), kind=kOutput, calls=%fused_computation.7 | convolution fusion | flops 1816608768 | bytes 11407872 | tf_op jit(solution)/shard_map/slcf,slcd->lfd/dot_general | solution.py:65
  297.7 8.4 %fusion.25 = (bf16[8,2,72]{2,0,1:T(8,128)(2,1)S(1)}, bf16[8,2,72,384]{3,2,0,1:T(8,128)(2,1)}, bf16[8,2,72,384]{3,2,0,1:T(8,128)(2,1)S(1)}) fusion(f32[2,8,72,384]{3,2,1,0:T(8,128)} %fusion.4, f32[2,8,72,384]{3,2,1,0:T(8,128)} %fusion.2, f32[8,2,72]{2,0,1:T(8,128)S(1)} %copy.53, bf16[2,384,2048]{2,1,0:T(8,128)(2,1)} %param.15, ...), kind=kOutput, calls=%fused_computation.43 | convolution fusion | flops 1819458432 | bytes 13179648 | tf_op jit(solution)/shard_map/slcd,lfd->slcf/dot_general | solution.py:56
  306.1 0.9 copy-done.4
  307.0 7.2 %bitcast_convert_fusion.1 = bf16[2,2048,384]{2,1,0:T(8,128)(2,1)} fusion(bf16[8,2,72,2048]{3,2,1,0:T(8,128)(2,1)} %bitcast.113, bf16[8,2,72,384]{3,2,0,1:T(8,128)(2,1)S(1)} %get-tuple-element.27), kind=kOutput, calls=%fused_computation.8 | convolution fusion | flops 1813512192 | bytes 8749056 | tf_op jit(solution)/shard_map/slcd,slcf->ldf/dot_general | solution.py:91
  314.3 0.7 convert_element_type.76
  315.0 3.3 all-to-all-start.4
  318.3 4.0 fusion.12
  322.3 4.2 fusion
  326.5 2.6 copy.57
  329.1 5.0 %all-to-all-start.3 = ((bf16[8,144,2048]{2,1,0:T(8,128)(2,1)}), bf16[8,144,2048]{2,1,0:T(8,128)(2,1)}, u32[]{:S(2)}, u32[]{:S(2)}) async-start(bf16[8,144,2048]{2,1,0:T(8,128)(2,1)} %bitcast.111), calls=%async_computation.3 | async-start | bytes 9437184 | tf_op jit(solution)/shard_map/all_to_all | solution.py:73
  334.4 7.5 %bitcast_convert_fusion.2 = bf16[2,2048,384]{2,1,0:T(8,128)(2,1)} fusion(bf16[8,2,72,2048]{3,2,1,0:T(8,128)(2,1)} %bitcast.114, bf16[8,2,72,384]{3,2,0,1:T(8,128)(2,1)} %get-tuple-element.26), kind=kOutput, calls=%fused_computation.9 | convolution fusion | flops 1813512192 | bytes 8749056 | tf_op jit(solution)/shard_map/slcd,slcf->ldf/dot_general | solution.py:88
  342.1 6.8 %gather_fusion.2 = bf16[1024]{0:T(1024)(128)(2,1)S(1)} fusion(bf16[1152]{0:T(1024)(128)(2,1)S(1)} %reshape.172, s32[1024]{0:T(1024)S(1)} %broadcast_clamp_fusion), kind=kCustom, calls=%fused_computation.4 | custom fusion | bytes 8192 | tf_op jit(solution)/shard_map/jit(_take)/gather | solution.py:87
  349.7 89.7 %all-to-all-done.3 = bf16[8,144,2048]{2,1,0:T(8,128)(2,1)} async-done(((bf16[8,144,2048]{2,1,0:T(8,128)(2,1)}), bf16[8,144,2048]{2,1,0:T(8,128)(2,1)}, u32[]{:S(2)}, u32[]{:S(2)}) %all-to-all-start.3) | async-done | bytes 4718624 | tf_op jit(solution)/shard_map/all_to_all | solution.py:73
  439.5 11.8 %gather_fusion.1 = bf16[1024,2048]{1,0:T(8,128)(2,1)} fusion(bf16[1152,2048]{1,0:T(8,128)(2,1)} %bitcast.20, s32[1024]{0:T(1024)S(1)} %broadcast_clamp_fusion), kind=kCustom, calls=%fused_computation.3 | custom fusion | bytes 8392704 | tf_op jit(solution)/shard_map/jit(_take)/gather | solution.py:84
  451.2 5.1 %fusion.1 = bf16[128,2048]{1,0:T(8,128)(2,1)} fusion(bf16[1024,2048]{1,0:T(8,128)(2,1)} %gather_fusion.1, pred[128,8]{1,0:T(8,128)(4,1)S(1)} %get-tuple-element.22), kind=kLoop, calls=%fused_computation.14 | loop fusion | flops 3932160 | bytes 4719616 | tf_op jit(solution)/shard_map/reduce_sum | solution.py:86
  (52 shorter events, 2.9 us)
Async XLA Ops:
  7.2 177.5 %copy-start = (bf16[2,2048,384]{2,1,0:T(8,128)(2,1)S(1)}, bf16[2,2048,384]{2,1,0:T(8,128)(2,1)}, u32[]{:S(2)}) copy-start(bf16[2,2048,384]{2,1,0:T(8,128)(2,1)} %param.13) | copy-start | bytes 9437188
  26.7 42.5 %all-to-all-start = ((bf16[8,1,144]{2,1,0:T(2,128)(2,1)}), bf16[8,1,144]{2,1,0:T(2,128)(2,1)S(1)}, u32[]{:S(2)}, u32[]{:S(2)}) async-start(bf16[8,1,144]{2,1,0:T(2,128)(2,1)} %select_n.75), calls=%async_computation | async-start | bytes 16384 | tf_op jit(solution)/shard_map/all_to_all | solution.py:46
  179.7 109.9 %all-to-all-start.1 = ((bf16[8,144,2048]{2,1,0:T(8,128)(2,1)}), bf16[8,144,2048]{2,1,0:T(8,128)(2,1)}, u32[]{:S(2)}, u32[]{:S(2)}) async-start(bf16[8,144,2048]{2,1,0:T(8,128)(2,1)} %bitcast.109), calls=%async_computation.1 | async-start | bytes 9437184 | tf_op jit(solution)/shard_map/all_to_all | solution.py:45
  184.3 272.1 %reduce-scatter.8.cloned.1.call-start = ((), (), s32[]{:S(2)}) async-start(), calls=%async_computation.10 | async-start | bytes 4718592 | tf_op jit(solution)/shard_map/reduce_scatter | solution.py:97
  184.6 6.3 %copy-start.1 = (bf16[8,144,2048]{2,1,0:T(8,128)(2,1)S(1)}, bf16[8,144,2048]{2,1,0:T(8,128)(2,1)}, u32[]{:S(2)}) copy-start(bf16[8,144,2048]{2,1,0:T(8,128)(2,1)} %all_to_all.27) | copy-start | bytes 14155780
  184.6 6.3 %copy-start.2 = (bf16[2,2048,384]{2,1,0:T(8,128)(2,1)S(1)}, bf16[2,2048,384]{2,1,0:T(8,128)(2,1)}, u32[]{:S(2)}) copy-start(bf16[2,2048,384]{2,1,0:T(8,128)(2,1)} %param.14) | copy-start | bytes 9437188
  297.4 158.9 %reduce-scatter.6.cloned.1.call-start = ((), (), s32[]{:S(2)}) async-start(), calls=%async_computation.9 | async-start | bytes 4718592 | tf_op jit(solution)/shard_map/reduce_scatter | solution.py:96
  306.1 0.9 copy-start.4
  315.0 14.1 %all-to-all-start.4 = ((bf16[8,1,144]{2,1,0:T(2,128)(2,1)}), bf16[8,1,144]{2,1,0:T(2,128)(2,1)S(1)}, u32[]{:S(2)}, u32[]{:S(2)}) async-start(bf16[8,1,144]{2,1,0:T(2,128)(2,1)} %convert_element_type.76), calls=%async_computation.4 | async-start | bytes 16384 | tf_op jit(solution)/shard_map/all_to_all | solution.py:76
  318.3 4.0 copy-start.3
  329.1 110.4 %all-to-all-start.3 = ((bf16[8,144,2048]{2,1,0:T(8,128)(2,1)}), bf16[8,144,2048]{2,1,0:T(8,128)(2,1)}, u32[]{:S(2)}, u32[]{:S(2)}) async-start(bf16[8,144,2048]{2,1,0:T(8,128)(2,1)} %bitcast.111), calls=%async_computation.3 | async-start | bytes 9437184 | tf_op jit(solution)/shard_map/all_to_all | solution.py:73
  334.1 122.3 %reduce-scatter.4.cloned.1.call-start = ((), (), s32[]{:S(2)}) async-start(), calls=%async_computation.8 | async-start | bytes 4718592 | tf_op jit(solution)/shard_map/reduce_scatter | solution.py:95
Sparse Core Ops, SparseCore 0:
  297.5 42.2 reduce-scatter.7
  342.7 43.3 reduce-scatter.5
  388.9 43.3 reduce-scatter.3
where the time goes:
time: 464 us; the launch traced here: 463 us
  waiting for transfers between devices  184 us (40%)
  blocking collectives  111 us (24%)
  local copies, waits for them, and re-layouts  65.9 us (14%)
  matrix products  49.3 us (11%)
  starting transfers between devices  20.1 us (4%)
  other arithmetic  18.7 us (4%)
  between operations  14 us (3%)
    all_to_all x1, blocking collectives, per_device(): lax.all_to_all(send_x, 'expert', split_axis=0, concat_axis=0, tiled=True)  111 us
    all_to_all x1, waiting for transfers between devices, per_device(): lax.all_to_all(send_dy, 'expert', split_axis=0, concat_axis=0, tiled=True)  94.7 us
    all_to_all x1, waiting for transfers between devices, per_device(): lax.all_to_all(row_grads.reshape(shape_rows), 'expert', split_axis=0, con...  89.7 us
    gather x1, local copies, waits for them, and re-layouts, per_device(): send_dy = jnp.take(padded_dy, owners, axis=0).reshape(shape_rows)  11.9 us
    gather x1, local copies, waits for them, and re-layouts, per_device(): jnp.take(back_rows.reshape(expert_count * capacity, feature_width), slot_...  11.8 us
    gather x1, local copies, waits for them, and re-layouts, per_device(): send_x = jnp.take(padded_x, owners, axis=0).reshape(shape_rows)  11.8 us
  transfers between devices with their start and end apart: 7, of which 2 were waited for; matrix products, arithmetic and copies ran while one was open for 23% of the time, Pallas kernels for 0%

commit v1 on v0

v1 whole, which is shorter than its diff:
```python
import jax
import jax.numpy as jnp
from jax import lax
from jax.sharding import PartitionSpec as P

BF = jnp.bfloat16
F32 = jnp.float32


def per_device(tokens, out_grads, routes, gates, gate_weight, up_weight, down_weight):
    tok_rows, width = tokens.shape
    top = routes.shape[1]
    local = gate_weight.shape[0]
    groups = lax.axis_size("expert")
    experts = local * groups
    cap = min(tok_rows, max(2, (tok_rows * top * 9 + experts * 8 - 1) // (experts * 8)))
    me = lax.axis_index("expert")

    names = jnp.arange(experts, dtype=jnp.int32)
    hit = routes[:, :, None] == names[None, None, :]
    gate_map = jnp.sum(jnp.where(hit, gates[:, :, None].astype(F32), 0.0), axis=1).astype(BF)

    all_map = lax.all_gather(gate_map, "expert", axis=0)
    all_x = lax.all_gather(tokens, "expert", axis=0)
    all_dy = lax.all_gather(out_grads, "expert", axis=0)

    mine = lax.dynamic_slice_in_dim(all_map, me * local, local, axis=2).transpose(2, 0, 1)
    used = mine > 0
    tri = jnp.triu(jnp.ones((tok_rows, tok_rows), BF))
    place = jnp.dot(used.astype(BF).reshape(-1, tok_rows), tri, preferred_element_type=F32)
    place = place.astype(jnp.int32).reshape(used.shape) - 1
    pick = (place[:, :, None, :] == jnp.arange(cap, dtype=jnp.int32)[None, None, :, None]) & used[:, :, None, :]
    pick = pick.astype(BF)
    gate_col = jnp.einsum("lsct,lst->lsc", pick, mine, preferred_element_type=F32)
    gate_col = gate_col.reshape(local, -1, 1)
    rows_x = jnp.einsum("lsct,std->lscd", pick, all_x, preferred_element_type=F32).astype(BF)
    rows_x = rows_x.reshape(local, groups * cap, width)
    pre_gate = jnp.einsum("lcd,ldf->lcf", rows_x, gate_weight, preferred_element_type=F32)
    pre_up = jnp.einsum("lcd,ldf->lcf", rows_x, up_weight, preferred_element_type=F32)
    sig = jax.nn.sigmoid(pre_gate)
    act = pre_gate * sig
    hidden = act * pre_up
    gated_hidden = (gate_col * hidden).astype(BF)
    rows_dy = jnp.einsum("lsct,std->lscd", pick, all_dy, preferred_element_type=F32).astype(BF)
    rows_dy = rows_dy.reshape(local, groups * cap, width)
    down_part = jnp.einsum("lcf,lcd->lfd", gated_hidden, rows_dy, preferred_element_type=F32).astype(BF)
    down_sum = lax.psum_scatter(down_part, "dp", scatter_dimension=2, tiled=True)
    back_raw = jnp.einsum("lcd,lfd->lcf", rows_dy, down_weight, preferred_element_type=F32)
    route_grad = jnp.sum(hidden * back_raw, axis=-1).astype(BF)
    back = gate_col * back_raw
    grad_gate = (back * pre_up * sig * (1.0 + pre_gate * (1.0 - sig))).astype(BF)
    grad_up = (back * act).astype(BF)
    gate_part = jnp.einsum("lcd,lcf->ldf", rows_x, grad_gate, preferred_element_type=F32).astype(BF)
    gate_sum = lax.psum_scatter(gate_part, "dp", scatter_dimension=1, tiled=True)
    up_part = jnp.einsum("lcd,lcf->ldf", rows_x, grad_up, preferred_element_type=F32).astype(BF)
    up_sum = lax.psum_scatter(up_part, "dp", scatter_dimension=1, tiled=True)

    row_grads = (
        jnp.einsum("lcf,ldf->lcd", grad_gate, gate_weight, preferred_element_type=F32)
        + jnp.einsum("lcf,ldf->lcd", grad_up, up_weight, preferred_element_type=F32)
    ).astype(BF).reshape(local, groups, cap, width)
    token_part = jnp.einsum("lsct,lscd->std", pick, row_grads, preferred_element_type=F32).astype(BF)
    input_grads = lax.psum_scatter(token_part, "expert", scatter_dimension=0, tiled=True)[0]

    back_route = jnp.einsum(
        "lsct,lsc->slt", pick, route_grad.reshape(local, groups, cap), preferred_element_type=F32
    ).astype(BF)
    own_route = lax.all_to_all(back_route, "expert", split_axis=0, concat_axis=0, tiled=True)
    own_route = own_route.reshape(experts, tok_rows).T.astype(F32)
    gate_grads = jnp.sum(jnp.where(hit, own_route[:, None, :], 0.0), axis=2).astype(BF)
    return (input_grads, gate_grads, gate_sum, up_sum, down_sum)


def solution(mesh):
    rows = P(("groups", "expert", "dp"), None)
    in_specs = (rows, rows, rows, rows, P("expert", None, None), P("expert", None, None), P("expert", None, None))
    out_specs = (
        rows,
        rows,
        P(("groups", "expert"), "dp", None),
        P(("groups", "expert"), "dp", None),
        P(("groups", "expert"), None, "dp"),
    )
    return jax.shard_map(per_device, mesh=mesh, in_specs=in_specs, out_specs=out_specs, check_vma=False)
```

time: 464 us -> 318 us (0.69)
  blocking collectives: 111 us -> 22.3 us
  local copies, waits for them, and re-layouts: 65.9 us -> 6.72 us
  waiting for transfers between devices: 184 us -> 220 us
  starting transfers between devices: 20.1 us -> 0.64 us
  other arithmetic: 18.7 us -> 2.01 us
    all_to_all x4 -> x0, waiting for transfers between devices: 184 us -> none  [the longest x1 94.7 us: per_device(): lax.all_to_all(send_dy, 'expert', split_axis=0, concat_axis=0, tiled=True)]
    all_to_all x1, blocking collectives: 111 us -> 7.92 us  [per_device(): lax.all_to_all(back_route, 'expert', split_axis=0, concat_axis=0, tiled=T...]
    reduce_scatter x1 -> x2, waiting for transfers between devices: 0.01 us -> 96.3 us  [the longest x1 52.9 us: per_device(): lax.psum_scatter(token_part, 'expert', scatter_dimension=0, tiled=True)[0]]
    all_gather x0 -> x2, waiting for transfers between devices: none -> 75.8 us  [the longest x1 41.5 us: per_device(): all_x = lax.all_gather(tokens, 'expert', axis=0)]
    gather x6 -> x0, local copies, waits for them, and re-layouts: 49.6 us -> none  [the longest x1 11.9 us: per_device(): send_dy = jnp.take(padded_dy, owners, axis=0).reshape(shape_rows)]
    reduce_scatter x1, waiting for transfers between devices: 0.01 us -> 46 us  [per_device(): lax.psum_scatter(gate_part, 'dp', scatter_dimension=1, tiled=True)]
    all_to_all x4 -> x0, starting transfers between devices: 19.3 us -> none  [the longest x1 6.33 us: per_device(): lax.all_to_all(send_gate, 'expert', split_axis=0, concat_axis=0, tiled=True)]
    all_gather x0 -> x1, blocking collectives: none -> 14.4 us  [per_device(): all_map = lax.all_gather(gate_map, 'expert', axis=0)]
  transfers between devices with their start and end apart: 7 -> 6, of which waited for: 2 -> 5; matrix products, arithmetic and copies ran while one was open for 23% -> 14% of each run, Pallas kernels for 0% -> 0%
where the time goes in v1:
time: 318 us; the launch traced here: 317 us
  waiting for transfers between devices  220 us (69%)
  matrix products  51.8 us (16%)
  blocking collectives  22.3 us (7%)
  between operations  14.3 us (4%)
  local copies, waits for them, and re-layouts  6.72 us (2%)
    reduce_scatter x1, waiting for transfers between devices, per_device(): lax.psum_scatter(token_part, 'expert', scatter_dimension=0, tiled=True)[0]  52.9 us
    reduce_scatter x1, waiting for transfers between devices, per_device(): lax.psum_scatter(gate_part, 'dp', scatter_dimension=1, tiled=True)  46 us
    reduce_scatter x1, waiting for transfers between devices, per_device(): up_sum = lax.psum_scatter(up_part, 'dp', scatter_dimension=1, tiled=True)  43.4 us
    all_gather x1, waiting for transfers between devices, per_device(): all_x = lax.all_gather(tokens, 'expert', axis=0)  41.5 us
    all_gather x1, waiting for transfers between devices, per_device(): all_dy = lax.all_gather(out_grads, 'expert', axis=0)  34.4 us
    all_gather x1, blocking collectives, per_device(): all_map = lax.all_gather(gate_map, 'expert', axis=0)  14.4 us
    dot_general x1, matrix products, per_device(): jnp.einsum('lcd,lfd->lcf', rows_dy, down_weight, preferred_element_type=F32)  8.42 us
    all_to_all x1, blocking collectives, per_device(): lax.all_to_all(back_route, 'expert', split_axis=0, concat_axis=0, tiled=T...  7.92 us
  transfers between devices with their start and end apart: 6, of which 5 were waited for; matrix products, arithmetic and copies ran while one was open for 14% of the time, Pallas kernels for 0%

profile of v1, /device:TPU:0, one launch (start us, length us, event | category | flops | bytes accessed | tf_op | source)
XLA Modules:
  0.0 317.4 jit_solution(12385354059392062342)
XLA Ops:
  7.2 0.7 all-gather.6.cloned.1.call-update
  8.0 0.7 all-gather.8.cloned.1.call-update
  8.7 0.7 convert_element_type.80
  9.4 0.7 select_reduce_fusion.1
  10.1 14.4 %all-gather = bf16[1024,16]{0,1:T(8,128)(2,1)S(1)} all-gather(bf16[128,16]{0,1:T(8,128)(2,1)S(1)} %select_reduce_fusion.1), channel_id=2, replica_groups=mesh['groups'=2,'expert'=8,'dp'=2] {'expert'}, dimensions={0}, use_global_device_ids=true | all-gather | bytes 36864 | tf_op jit(solution)/shard_map/all_gather | solution.py:23
  24.8 0.3 fusion.10
  25.1 34.4 %all-gather.6.cloned.1.call-done = bf16[1024,2048]{1,0:T(8,128)(2,1)} async-done(((bf16[128,2048]{1,0:T(8,128)(2,1)}), bf16[1024,2048]{1,0:T(8,128)(2,1)}) %all-gather.6.cloned.1.call-update) | async-done | bytes 4194320 | tf_op jit(solution)/shard_map/all_gather | solution.py:25
  59.5 3.6 %convert_bitcast_fusion.1 = bf16[2,8,72,2048]{3,2,0,1:T(8,128)(2,1)S(1)} fusion(bf16[8,128,2048,1]{2,1,3,0:T(8,128)(2,1)} %bitcast.61, s32[2,8,128]{2,0,1:T(2,128)S(1)} %copy.24, pred[2,8,128]{2,0,1:T(4,128)(4,1)S(1)} %copy.25), kind=kOutput, calls=%fused_computation.5 | convolution fusion | flops 606633984 | bytes 8923136 | tf_op jit(solution)/shard_map/lsct,std->lscd/dot_general | solution.py:44
  63.1 2.6 copy.26
  65.6 41.5 %all-gather.8.cloned.1.call-done = bf16[1024,2048]{1,0:T(8,128)(2,1)} async-done(((bf16[128,2048]{1,0:T(8,128)(2,1)}), bf16[1024,2048]{1,0:T(8,128)(2,1)}) %all-gather.8.cloned.1.call-update) | async-done | bytes 4194320 | tf_op jit(solution)/shard_map/all_gather | solution.py:24
  107.1 3.6 %convert_bitcast_fusion = bf16[2,8,72,2048]{3,2,0,1:T(8,128)(2,1)S(1)} fusion(bf16[8,128,2048,1]{2,1,3,0:T(8,128)(2,1)} %bitcast.62, s32[2,8,128]{2,0,1:T(2,128)S(1)} %copy.24, pred[2,8,128]{2,0,1:T(4,128)(4,1)S(1)} %copy.25), kind=kOutput, calls=%fused_computation.4 | convolution fusion | flops 606633984 | bytes 8923136 | tf_op jit(solution)/shard_map/lsct,std->lscd/dot_general | solution.py:36
  110.6 0.7 copy.27
  111.4 2.6 fusion.29
  114.0 0.9 copy-done.2
  115.0 2.6 fusion.28
  117.6 1.2 copy-done.7
  118.9 4.4 %convolution_convert_fusion = bf16[2,384,2048]{2,1,0:T(8,128)(2,1)} fusion(bf16[2,576,2048]{2,1,0:T(8,128)(2,1)S(1)} %bitcast.70, f32[2,576]{1,0:T(2,128)S(1)} %mul.44, f32[2,576,384]{2,1,0:T(8,128)S(1)} %fusion.28, f32[2,576,384]{2,1,0:T(8,128)S(1)} %fusion.29), kind=kOutput, calls=%fused_computation.6 | convolution fusion | flops 1816608768 | bytes 11407872 | tf_op jit(solution)/shard_map/lcf,lcd->lfd/dot_general | solution.py:46
  123.3 0.2 reduce-scatter.9.cloned.1.call-start
  123.5 8.4 %multiply_reduce_fusion = (bf16[2,576]{1,0:T(2,128)(2,1)S(1)}, bf16[2,576,384]{2,1,0:T(8,128)(2,1)}, bf16[2,576,384]{2,1,0:T(8,128)(2,1)S(1)}) fusion(f32[2,576,384]{2,1,0:T(8,128)} %copy-done.7, f32[2,576,384]{2,1,0:T(8,128)} %copy-done.6, f32[2,576]{1,0:T(2,128)S(1)} %mul.44, bf16[2,576,2048]{2,1,0:T(8,128)(2,1)} %bitcast.67, bf16[2,384,2048]{2,1,0:T(8,128)(2,1)} %param.13), kind=kOutput, calls=%fused_computation.10 | convolution fusion | flops 1819458432 | bytes 13179648 | tf_op jit(solution)/shard_map/lcd,lfd->lcf/dot_general | solution.py:48
  131.9 1.0 copy-done.4
  132.9 7.2 %convolution_convert_fusion.1 = bf16[2,2048,384]{2,1,0:T(8,128)(2,1)} fusion(bf16[2,576,2048]{2,1,0:T(8,128)(2,1)} %bitcast.65, bf16[2,576,384]{2,1,0:T(8,128)(2,1)S(1)} %get-tuple-element.7), kind=kOutput, calls=%fused_computation.7 | convolution fusion | flops 1813512192 | bytes 8749056 | tf_op jit(solution)/shard_map/lcd,lcf->ldf/dot_general | solution.py:55
  140.2 7.5 %convolution_convert_fusion.2 = bf16[2,2048,384]{2,1,0:T(8,128)(2,1)} fusion(bf16[2,576,2048]{2,1,0:T(8,128)(2,1)} %bitcast.66, bf16[2,576,384]{2,1,0:T(8,128)(2,1)} %get-tuple-element.6), kind=kOutput, calls=%fused_computation.8 | convolution fusion | flops 1813512192 | bytes 8749056 | tf_op jit(solution)/shard_map/lcd,lcf->ldf/dot_general | solution.py:53
  147.6 0.3 reduce-scatter.5.cloned.1.call-start
  147.9 4.0 %fusion.30 = f32[2,576,2048]{2,1,0:T(8,128)S(1)} fusion(bf16[2,576,384]{2,1,0:T(8,128)(2,1)} %get-tuple-element.6, bf16[2,2048,384]{2,1,0:T(8,128)(2,1)S(1)} %copy-done), kind=kOutput, calls=%fused_computation.44 | convolution fusion | flops 1811939328 | bytes 13467648 | tf_op jit(solution)/shard_map/lcf,ldf->lcd/dot_general | solution.py:59
  151.9 4.1 %add_convert_fusion = bf16[2,576,2048]{2,1,0:T(8,128)(2,1)S(1)} fusion(f32[2,576,2048]{2,1,0:T(8,128)S(1)} %fusion.30, bf16[2,576,384]{2,1,0:T(8,128)(2,1)} %copy-done.4, bf16[2,2048,384]{2,1,0:T(8,128)(2,1)S(1)} %copy-done.3), kind=kOutput, calls=%fused_computation | convolution fusion | flops 1816657920 | bytes 18186240 | tf_op jit(solution)/shard_map/lcf,ldf->lcd/dot_general | solution.py:60
  156.1 3.3 %bitcast_convert_fusion = bf16[8,128,2048]{2,1,0:T(8,128)(2,1)} fusion(bf16[2,8,72,2048]{3,2,1,0:T(8,128)(2,1)S(1)} %bitcast.60, s32[2,8,128]{2,0,1:T(2,128)S(1)} %copy.24, pred[2,8,128]{2,0,1:T(4,128)(4,1)S(1)} %copy.25), kind=kOutput, calls=%fused_computation.1 | convolution fusion | flops 606371840 | bytes 8923136 | tf_op jit(solution)/shard_map/lsct,lscd->std/dot_general | solution.py:62
  159.4 0.2 fusion.18
  159.7 7.9 %all_to_all.5 = bf16[8,2,128]{2,1,0:T(2,128)(2,1)S(1)} all-to-all(bf16[8,2,128]{2,1,0:T(2,128)(2,1)S(1)} %convert_element_type.94), channel_id=1, replica_groups=mesh['groups'=2,'expert'=8,'dp'=2] {'expert'}, dimensions={0} | all-to-all | bytes 8192 | tf_op jit(solution)/shard_map/all_to_all | solution.py:68
  167.6 0.6 select_reduce_fusion
  168.2 43.4 %reduce-scatter.9.cloned.1.call-done = bf16[2,1024,384]{2,1,0:T(8,128)(2,1)} async-done(((bf16[2,2048,384]{2,1,0:T(8,128)(2,1)}), bf16[2,1024,384]{2,1,0:T(8,128)(2,1)}) %reduce-scatter.9.cloned.1.call-update) | async-done | bytes 1572880 | tf_op jit(solution)/shard_map/reduce_scatter | solution.py:56
  211.6 46.0 %reduce-scatter.7.cloned.1.call-done = bf16[2,1024,384]{2,1,0:T(8,128)(2,1)} async-done(((bf16[2,2048,384]{2,1,0:T(8,128)(2,1)}), bf16[2,1024,384]{2,1,0:T(8,128)(2,1)}) %reduce-scatter.7.cloned.1.call-update) | async-done | bytes 1572880 | tf_op jit(solution)/shard_map/reduce_scatter | solution.py:54
  257.7 52.9 %reduce-scatter.5.cloned.1.call-done = bf16[1,128,2048]{2,1,0:T(8,128)(2,1)} async-done(((bf16[8,128,2048]{2,1,0:T(8,128)(2,1)}), bf16[1,128,2048]{2,1,0:T(8,128)(2,1)}) %reduce-scatter.5.cloned.1.call-update) | async-done | bytes 524304 | tf_op jit(solution)/shard_map/reduce_scatter | solution.py:63
  (38 shorter events, 0.7 us)
Async XLA Ops:
  7.2 104.2 %copy-start = (bf16[2,2048,384]{2,1,0:T(8,128)(2,1)S(1)}, bf16[2,2048,384]{2,1,0:T(8,128)(2,1)}, u32[]{:S(2)}) copy-start(bf16[2,2048,384]{2,1,0:T(8,128)(2,1)} %param.11) | copy-start | bytes 9437188
  7.2 52.3 %all-gather.6.cloned.1.call-start = ((), (), s32[]{:S(2)}) async-start(), calls=%async_computation.9 | async-start | bytes 4718592 | tf_op jit(solution)/shard_map/all_gather | solution.py:25
  7.9 99.2 %all-gather.8.cloned.1.call-start = ((), (), s32[]{:S(2)}) async-start(), calls=%async_computation.10 | async-start | bytes 4718592 | tf_op jit(solution)/shard_map/all_gather | solution.py:24
  8.7 159.5 %reduce-scatter.11.cloned.1.call-start = ((), (), s32[]{:S(2)}) async-start(), calls=%async_computation.8 | async-start | bytes 4718592 | tf_op jit(solution)/shard_map/reduce_scatter | solution.py:47
  111.4 2.7 copy-start.1
  111.4 3.6 %copy-start.2 = (bf16[2,2048,384]{2,1,0:T(8,128)(2,1)S(1)}, bf16[2,2048,384]{2,1,0:T(8,128)(2,1)}, u32[]{:S(2)}) copy-start(bf16[2,2048,384]{2,1,0:T(8,128)(2,1)} %param.12) | copy-start | bytes 9437188
  111.4 7.5 %slice-start = ((s8[4718592]{0:T(1024)(128)(4,1)}), s8[4194304]{0:T(1024)(128)(4,1)S(1)}, s32[]{:S(2)}) async-start(s8[4718592]{0:T(1024)(128)(4,1)} %bitcast.68), calls=%async_computation.11 | async-start | bytes 8388608
  115.0 2.6 copy-start.6
  115.0 3.9 %slice-start.1 = ((s8[4718592]{0:T(1024)(128)(4,1)}), s8[524288]{0:T(1024)(128)(4,1)S(1)}, s32[]{:S(2)}) async-start(s8[4718592]{0:T(1024)(128)(4,1)} %bitcast.68), calls=%async_computation.12 | async-start | bytes 1048576
  117.6 1.3 copy-start.7
  123.3 88.4 %reduce-scatter.9.cloned.1.call-start = ((), (), s32[]{:S(2)}) async-start(), calls=%async_computation.7 | async-start | bytes 4718592 | tf_op jit(solution)/shard_map/reduce_scatter | solution.py:56
  131.9 1.0 copy-start.4
  140.1 117.6 %reduce-scatter.7.cloned.1.call-start = ((), (), s32[]{:S(2)}) async-start(), calls=%async_computation.6 | async-start | bytes 4718592 | tf_op jit(solution)/shard_map/reduce_scatter | solution.py:54
  147.6 162.9 %reduce-scatter.5.cloned.1.call-start = ((), (), s32[]{:S(2)}) async-start(), calls=%async_computation.5 | async-start | bytes 4718592 | tf_op jit(solution)/shard_map/reduce_scatter | solution.py:63
  147.9 4.0 %copy-start.3 = (bf16[2,2048,384]{2,1,0:T(8,128)(2,1)S(1)}, bf16[2,2048,384]{2,1,0:T(8,128)(2,1)}, u32[]{:S(2)}) copy-start(bf16[2,2048,384]{2,1,0:T(8,128)(2,1)} %param.12) | copy-start | bytes 9437188
  159.3 8.3 %copy-start.5 = (s32[128,8]{0,1:T(8,128)S(1)}, s32[128,8]{0,1:T(8,128)}, u32[]{:S(2)}) copy-start(s32[128,8]{0,1:T(8,128)} %param.9) | copy-start | bytes 12292
Sparse Core Ops, SparseCore 0:
  9.6 49.8 all-gather.5
  61.1 45.9 all-gather.7
  123.4 42.0 reduce-scatter.10
  168.2 43.3 reduce-scatter.8
  214.3 43.3 reduce-scatter.6
  260.5 50.0 reduce-scatter.4

commit v2 on v1

--- a/solution.py
+++ b/solution.py
@@ -5,6 +5,24 @@
 
 BF = jnp.bfloat16
 F32 = jnp.float32
+
+
+def halves(rows):
+    if lax.axis_size("dp") != 2:
+        return rows, rows
+    at, width = lax.axis_index("dp"), rows.shape[-1] // 2
+    return (
+        lax.dynamic_slice_in_dim(rows, (1 - at) * width, width, axis=-1),
+        lax.dynamic_slice_in_dim(rows, at * width, width, axis=-1),
+    )
+
+
+def replica_sum(grad, give, keep, dim):
+    if lax.axis_size("dp") != 2:
+        return lax.psum_scatter(grad(keep).astype(BF), "dp", scatter_dimension=dim, tiled=True)
+    other = lax.ppermute(grad(give).astype(BF), "dp", [(0, 1), (1, 0)])
+    own = grad(keep).astype(BF)
+    return (own.astype(F32) + other.astype(F32)).astype(BF)
 
 
 def per_device(tokens, out_grads, routes, gates, gate_weight, up_weight, down_weight):
@@ -43,17 +61,16 @@
     gated_hidden = (gate_col * hidden).astype(BF)
     rows_dy = jnp.einsum("lsct,std->lscd", pick, all_dy, preferred_element_type=F32).astype(BF)
     rows_dy = rows_dy.reshape(local, groups * cap, width)
-    down_part = jnp.einsum("lcf,lcd->lfd", gated_hidden, rows_dy, preferred_element_type=F32).astype(BF)
-    down_sum = lax.psum_scatter(down_part, "dp", scatter_dimension=2, tiled=True)
+    give_dy, keep_dy = halves(rows_dy)
+    down_sum = replica_sum(lambda d: jnp.einsum("lcf,lcd->lfd", gated_hidden, d, preferred_element_type=F32), give_dy, keep_dy, 2)
     back_raw = jnp.einsum("lcd,lfd->lcf", rows_dy, down_weight, preferred_element_type=F32)
     route_grad = jnp.sum(hidden * back_raw, axis=-1).astype(BF)
     back = gate_col * back_raw
     grad_gate = (back * pre_up * sig * (1.0 + pre_gate * (1.0 - sig))).astype(BF)
     grad_up = (back * act).astype(BF)
-    gate_part = jnp.einsum("lcd,lcf->ldf", rows_x, grad_gate, preferred_element_type=F32).astype(BF)
-    gate_sum = lax.psum_scatter(gate_part, "dp", scatter_dimension=1, tiled=True)
-    up_part = jnp.einsum("lcd,lcf->ldf", rows_x, grad_up, preferred_element_type=F32).astype(BF)
-    up_sum = lax.psum_scatter(up_part, "dp", scatter_dimension=1, tiled=True)
+    give_x, keep_x = halves(rows_x)
+    gate_sum = replica_sum(lambda d: jnp.einsum("lcd,lcf->ldf", d, grad_gate, preferred_element_type=F32), give_x, keep_x, 1)
+    up_sum = replica_sum(lambda d: jnp.einsum("lcd,lcf->ldf", d, grad_up, preferred_element_type=F32), give_x, keep_x, 1)
 
     row_grads = (
         jnp.einsum("lcf,ldf->lcd", grad_gate, gate_weight, preferred_element_type=F32)

time: 318 us -> 254 us (0.80)
  waiting for transfers between devices: 220 us -> 154 us
  blocking collectives: 22.3 us -> 14.4 us
  starting transfers between devices: 0.64 us -> 7.15 us
  matrix products: 51.8 us -> 56.3 us
    reduce_scatter x3 -> x0, waiting for transfers between devices: 89.5 us -> none  [the longest x1 46 us: per_device(): lax.psum_scatter(gate_part, 'dp', scatter_dimension=1, tiled=True)]
    ppermute x0 -> x3, waiting for transfers between devices: none -> 71.3 us  [replica_sum(): other = lax.ppermute(grad(give).astype(BF), 'dp', [(0, 1), (1, 0)])]
    reduce_scatter x1, waiting for transfers between devices: 52.9 us -> 0.01 us  [per_device(): lax.psum_scatter(token_part, 'expert', scatter_dimension=0, tiled=True)[0]]
    dot_general x3 -> x6, matrix products: 19 us -> 28.2 us  [the longest x2 9.67 us: per_device(): jnp.einsum('lcd,lcf->ldf', d, grad_gate, preferred_element_type=F32)]
    all_to_all x1 -> x0, blocking collectives: 7.92 us -> none  [per_device(): lax.all_to_all(back_route, 'expert', split_axis=0, concat_axis=0, tiled=T...]
    all_to_all x0 -> x1, waiting for transfers between devices: none -> 5.33 us  [per_device(): lax.all_to_all(back_route, 'expert', split_axis=0, concat_axis=0, tiled=T...]
    dot_general x1, matrix products: 8.42 us -> 4.71 us  [per_device(): jnp.einsum('lcd,lfd->lcf', rows_dy, down_weight, preferred_element_type=F32)]
    all_to_all x0 -> x1, starting transfers between devices: none -> 3.54 us  [per_device(): lax.all_to_all(back_route, 'expert', split_axis=0, concat_axis=0, tiled=T...]
  transfers between devices with their start and end apart: 6 -> 7, of which waited for: 5 -> 6; matrix products, arithmetic and copies ran while one was open for 14% -> 15% of each run, Pallas kernels for 0% -> 0%
where the time goes in v2:
time: 254 us
  waiting for transfers between devices  154 us (61%)
  matrix products  56.3 us (22%)
  blocking collectives  14.4 us (6%)
  between operations  14 us (6%)
  starting transfers between devices  7.15 us (3%)
  local copies, waits for them, and re-layouts  5.45 us (2%)
  other arithmetic  2.6 us (1%)
    ppermute x3, waiting for transfers between devices, replica_sum(): other = lax.ppermute(grad(give).astype(BF), 'dp', [(0, 1), (1, 0)])  71.3 us
    all_gather x1, waiting for transfers between devices, per_device(): all_x = lax.all_gather(tokens, 'expert', axis=0)  41.5 us
    all_gather x1, waiting for transfers between devices, per_device(): all_dy = lax.all_gather(out_grads, 'expert', axis=0)  34.3 us
    all_gather x1, blocking collectives, per_device(): all_map = lax.all_gather(gate_map, 'expert', axis=0)  14.4 us
    dot_general x2, matrix products, per_device(): jnp.einsum('lcd,lcf->ldf', d, grad_gate, preferred_element_type=F32)  9.67 us
    dot_general x2, matrix products, per_device(): jnp.einsum('lcd,lcf->ldf', d, grad_up, preferred_element_type=F32)  9.55 us
    dot_general x2, matrix products, per_device(): jnp.einsum('lcf,lcd->lfd', gated_hidden, d, preferred_element_type=F32)  9 us
    all_to_all x1, waiting for transfers between devices, per_device(): lax.all_to_all(back_route, 'expert', split_axis=0, concat_axis=0, tiled=T...  5.33 us
  transfers between devices with their start and end apart: 7, of which 6 were waited for; matrix products, arithmetic and copies ran while one was open for 15% of the time, Pallas kernels for 0%

profile of v2, /device:TPU:0, one launch (start us, length us, event | category | flops | bytes accessed | tf_op | source)
XLA Modules:
  0.0 253.8 jit_solution(10371151717681319575)
XLA Ops:
  7.2 0.7 all-gather.6.cloned.1.call-update
  8.0 0.7 all-gather.8.cloned.1.call-update
  8.7 0.7 convert_element_type.116
  9.4 0.7 select_reduce_fusion.1
  10.1 14.4 %all-gather = bf16[1024,16]{0,1:T(8,128)(2,1)S(1)} all-gather(bf16[128,16]{0,1:T(8,128)(2,1)S(1)} %select_reduce_fusion.1), channel_id=2, replica_groups=mesh['groups'=2,'expert'=8,'dp'=2] {'expert'}, dimensions={0}, use_global_device_ids=true | all-gather | bytes 36864 | tf_op jit(solution)/shard_map/all_gather | solution.py:41
  25.1 34.3 %all-gather.6.cloned.1.call-done = bf16[1024,2048]{1,0:T(8,128)(2,1)} async-done(((bf16[128,2048]{1,0:T(8,128)(2,1)}), bf16[1024,2048]{1,0:T(8,128)(2,1)}) %all-gather.6.cloned.1.call-update) | async-done | bytes 4194320 | tf_op jit(solution)/shard_map/all_gather | solution.py:43
  59.5 3.6 %convert_bitcast_fusion.1 = bf16[2,8,72,2048]{3,2,0,1:T(8,128)(2,1)S(1)} fusion(bf16[8,128,2048,1]{2,1,3,0:T(8,128)(2,1)} %bitcast.62, s32[2,8,128]{2,0,1:T(2,128)S(1)} %copy.24, pred[2,8,128]{2,0,1:T(4,128)(4,1)S(1)} %copy.25), kind=kOutput, calls=%fused_computation.5 | convolution fusion | flops 606633984 | bytes 8923136 | tf_op jit(solution)/shard_map/lsct,std->lscd/dot_general | solution.py:62
  63.1 2.5 copy.26
  65.6 41.5 %all-gather.8.cloned.1.call-done = bf16[1024,2048]{1,0:T(8,128)(2,1)} async-done(((bf16[128,2048]{1,0:T(8,128)(2,1)}), bf16[1024,2048]{1,0:T(8,128)(2,1)}) %all-gather.8.cloned.1.call-update) | async-done | bytes 4194320 | tf_op jit(solution)/shard_map/all_gather | solution.py:42
  107.1 3.6 %convert_bitcast_fusion = bf16[2,8,72,2048]{3,2,0,1:T(8,128)(2,1)S(1)} fusion(bf16[8,128,2048,1]{2,1,3,0:T(8,128)(2,1)} %bitcast.63, s32[2,8,128]{2,0,1:T(2,128)S(1)} %copy.24, pred[2,8,128]{2,0,1:T(4,128)(4,1)S(1)} %copy.25), kind=kOutput, calls=%fused_computation.4 | convolution fusion | flops 606633984 | bytes 8923136 | tf_op jit(solution)/shard_map/lsct,std->lscd/dot_general | solution.py:54
  110.6 0.6 copy.27
  111.3 2.6 %fusion.68 = f32[2,576,384]{2,1,0:T(8,128)S(1)} fusion(bf16[2,576,2048]{2,1,0:T(8,128)(2,1)S(1)} %bitcast.69, bf16[2,2048,384]{2,1,0:T(8,128)(2,1)S(1)} %copy-done), kind=kOutput, calls=%fused_computation.65 | convolution fusion | flops 1811939328 | bytes 9633792 | tf_op jit(solution)/shard_map/lcd,ldf->lcf/dot_general | solution.py:56
  113.9 0.9 copy-done.3
  114.9 2.6 %fusion.67 = f32[2,576,384]{2,1,0:T(8,128)S(1)} fusion(bf16[2,576,2048]{2,1,0:T(8,128)(2,1)S(1)} %bitcast.70, bf16[2,2048,384]{2,1,0:T(8,128)(2,1)S(1)} %copy-done.3), kind=kOutput, calls=%fused_computation.64 | convolution fusion | flops 1811939328 | bytes 9633792 | tf_op jit(solution)/shard_map/lcd,ldf->lcf/dot_general | solution.py:57
  117.5 4.7 %multiply_reduce_fusion = (bf16[2,576]{1,0:T(2,128)(2,1)S(1)}, bf16[2,576,384]{2,1,0:T(8,128)(2,1)S(1)}, bf16[2,576,384]{2,1,0:T(8,128)(2,1)}, bf16[2,576,384]{2,1,0:T(8,128)(2,1)}) fusion(f32[2,576,384]{2,1,0:T(8,128)S(1)} %fusion.67, f32[2,576,384]{2,1,0:T(8,128)S(1)} %fusion.68, f32[2,576]{1,0:T(2,128)S(1)} %mul.52, ...), kind=kOutput, calls=%fused_computation.22 | convolution fusion | flops 1820343168 | bytes 14064384 | tf_op jit(solution)/shard_map/lcd,lfd->lcf/dot_general | solution.py:66
  122.2 2.8 %fusion.69 = f32[2,576,2048]{2,1,0:T(8,128)S(1)} fusion(bf16[2,576,384]{2,1,0:T(8,128)(2,1)S(1)} %get-tuple-element.6, bf16[2,2048,384]{2,1,0:T(8,128)(2,1)S(1)} %copy-done), kind=kOutput, calls=%fused_computation.66 | convolution fusion | flops 1811939328 | bytes 13467648 | tf_op jit(solution)/shard_map/lcf,ldf->lcd/dot_general | solution.py:76
  125.1 4.1 %add_convert_fusion = bf16[2,576,2048]{2,1,0:T(8,128)(2,1)S(1)} fusion(f32[2,576,2048]{2,1,0:T(8,128)S(1)} %fusion.69, bf16[2,576,384]{2,1,0:T(8,128)(2,1)} %get-tuple-element.8, bf16[2,2048,384]{2,1,0:T(8,128)(2,1)S(1)} %copy-done.3), kind=kOutput, calls=%fused_computation | convolution fusion | flops 1816657920 | bytes 18186240 | tf_op jit(solution)/shard_map/lcf,ldf->lcd/dot_general | solution.py:77
  129.2 3.4 %bitcast_convert_fusion = bf16[8,128,2048]{2,1,0:T(8,128)(2,1)} fusion(bf16[2,8,72,2048]{3,2,1,0:T(8,128)(2,1)S(1)} %bitcast.61, s32[2,8,128]{2,0,1:T(2,128)S(1)} %copy.24, pred[2,8,128]{2,0,1:T(4,128)(4,1)S(1)} %copy.25), kind=kOutput, calls=%fused_computation.1 | convolution fusion | flops 606371840 | bytes 8923136 | tf_op jit(solution)/shard_map/lsct,lscd->std/dot_general | solution.py:79
  132.6 1.1 copy-done.7
  133.8 4.5 %fusion.26 = bf16[2,1024,384]{2,1,0:T(8,128)(2,1)} fusion(bf16[2,576,384]{2,1,0:T(8,128)(2,1)S(1)} %copy-done.7, bf16[2,576,2048]{2,1,0:T(8,128)(2,1)} %bitcast.71, s32[]{:T(128)S(6)} %select_n.28), kind=kOutput, calls=%fused_computation.30 | convolution fusion | flops 906756096 | bytes 4816900 | tf_op jit(solution)/shard_map/lcd,lcf->ldf/dot_general | solution.py:73
  138.3 1.5 collective-permute-start.1
  139.8 4.5 %fusion.23 = bf16[2,1024,384]{2,1,0:T(8,128)(2,1)} fusion(bf16[2,576,384]{2,1,0:T(8,128)(2,1)S(1)} %copy-done.5, bf16[2,576,2048]{2,1,0:T(8,128)(2,1)} %bitcast.72, s32[]{:T(128)S(6)} %select_n.28), kind=kOutput, calls=%fused_computation.29 | convolution fusion | flops 906756096 | bytes 4816900 | tf_op jit(solution)/shard_map/lcd,lcf->ldf/dot_general | solution.py:72
  144.8 4.3 %fusion.32 = bf16[2,384,1024]{2,1,0:T(8,128)(2,1)} fusion(bf16[2,576,384]{2,1,0:T(8,128)(2,1)S(1)} %copy-done.10, bf16[2,576,2048]{2,1,0:T(8,128)(2,1)} %bitcast.64, s32[]{:T(128)S(6)} %select_n.28), kind=kOutput, calls=%fused_computation.32 | convolution fusion | flops 906756096 | bytes 4816900 | tf_op jit(solution)/shard_map/lcf,lcd->lfd/dot_general | solution.py:65
  149.1 1.5 collective-permute-start.2
  151.5 3.5 %all-to-all-start = ((bf16[8,2,128]{2,1,0:T(2,128)(2,1)}), bf16[8,2,128]{2,1,0:T(2,128)(2,1)S(1)}, u32[]{:S(2)}, u32[]{:S(2)}) async-start(bf16[8,2,128]{2,1,0:T(2,128)(2,1)} %convert_element_type.130), calls=%async_computation.1 | async-start | bytes 8192 | tf_op jit(solution)/shard_map/all_to_all | solution.py:85
  155.1 5.3 %all-to-all-done = bf16[8,2,128]{2,1,0:T(2,128)(2,1)S(1)} async-done(((bf16[8,2,128]{2,1,0:T(2,128)(2,1)}), bf16[8,2,128]{2,1,0:T(2,128)(2,1)S(1)}, u32[]{:S(2)}, u32[]{:S(2)}) %all-to-all-start) | async-done | bytes 4128 | tf_op jit(solution)/shard_map/all_to_all | solution.py:85
  161.0 14.8 %collective-permute-done.1 = bf16[2,1024,384]{2,1,0:T(8,128)(2,1)} collective-permute-done((bf16[2,1024,384]{2,1,0:T(8,128)(2,1)}, bf16[2,1024,384]{2,1,0:T(8,128)(2,1)}, u32[]{:S(2)}, u32[]{:S(2)}) %collective-permute-start.1) | collective-permute-done | bytes 1572896 | tf_op jit(solution)/shard_map/ppermute | solution.py:23
  175.8 5.0 %add_convert_fusion.2 = bf16[2,1024,384]{2,1,0:T(8,128)(2,1)} fusion(bf16[2,1024,384]{2,1,0:T(8,128)(2,1)} %collective-permute-done.1, bf16[2,576,384]{2,1,0:T(8,128)(2,1)S(1)} %copy-done.7, bf16[2,576,2048]{2,1,0:T(8,128)(2,1)} %bitcast.73, s32[]{:T(128)S(6)} %select_n.27), kind=kOutput, calls=%fused_computation.7 | convolution fusion | flops 909901824 | bytes 6389764 | tf_op jit(solution)/shard_map/lcd,lcf->ldf/dot_general | solution.py:73
  180.9 28.7 %collective-permute-done = bf16[2,1024,384]{2,1,0:T(8,128)(2,1)} collective-permute-done((bf16[2,1024,384]{2,1,0:T(8,128)(2,1)}, bf16[2,1024,384]{2,1,0:T(8,128)(2,1)}, u32[]{:S(2)}, u32[]{:S(2)}) %collective-permute-start) | collective-permute-done | bytes 1572896 | tf_op jit(solution)/shard_map/ppermute | solution.py:23
  209.5 5.2 %add_convert_fusion.3 = bf16[2,1024,384]{2,1,0:T(8,128)(2,1)} fusion(bf16[2,1024,384]{2,1,0:T(8,128)(2,1)} %collective-permute-done, bf16[2,576,384]{2,1,0:T(8,128)(2,1)S(1)} %copy-done.6, bf16[2,576,2048]{2,1,0:T(8,128)(2,1)} %bitcast.74, s32[]{:T(128)S(6)} %select_n.27), kind=kOutput, calls=%fused_computation.8 | convolution fusion | flops 909901824 | bytes 6389764 | tf_op jit(solution)/shard_map/lcd,lcf->ldf/dot_general | solution.py:72
  214.7 27.9 %collective-permute-done.2 = bf16[2,384,1024]{2,1,0:T(8,128)(2,1)} collective-permute-done((bf16[2,384,1024]{2,1,0:T(8,128)(2,1)}, bf16[2,384,1024]{2,1,0:T(8,128)(2,1)}, u32[]{:S(2)}, u32[]{:S(2)}) %collective-permute-start.2) | collective-permute-done | bytes 1572896 | tf_op jit(solution)/shard_map/ppermute | solution.py:23
  242.6 4.7 %add_convert_fusion.1 = bf16[2,384,1024]{2,1,0:T(8,128)(2,1)} fusion(bf16[2,384,1024]{2,1,0:T(8,128)(2,1)} %collective-permute-done.2, bf16[2,576,384]{2,1,0:T(8,128)(2,1)S(1)} %copy-done.11, bf16[2,576,2048]{2,1,0:T(8,128)(2,1)} %bitcast.65, s32[]{:T(128)S(6)} %select_n.27), kind=kOutput, calls=%fused_computation.6 | convolution fusion | flops 909901824 | bytes 6389764 | tf_op jit(solution)/shard_map/lcf,lcd->lfd/dot_general | solution.py:65
  (47 shorter events, 2.9 us)
Async XLA Ops:
  7.2 104.1 %copy-start = (bf16[2,2048,384]{2,1,0:T(8,128)(2,1)S(1)}, bf16[2,2048,384]{2,1,0:T(8,128)(2,1)}, u32[]{:S(2)}) copy-start(bf16[2,2048,384]{2,1,0:T(8,128)(2,1)} %param.11) | copy-start | bytes 9437188
  7.2 52.3 %all-gather.6.cloned.1.call-start = ((), (), s32[]{:S(2)}) async-start(), calls=%async_computation.3 | async-start | bytes 4718592 | tf_op jit(solution)/shard_map/all_gather | solution.py:43
  7.9 99.2 %all-gather.8.cloned.1.call-start = ((), (), s32[]{:S(2)}) async-start(), calls=%async_computation.4 | async-start | bytes 4718592 | tf_op jit(solution)/shard_map/all_gather | solution.py:42
  8.7 238.6 %reduce-scatter.2.cloned.1.call-start = ((), (), s32[]{:S(2)}) async-start(), calls=%async_computation.2 | async-start | bytes 4718592 | tf_op jit(solution)/shard_map/reduce_scatter | solution.py:80
  111.3 2.7 %copy-start.2 = (bf16[2,8,72,2048]{3,2,1,0:T(8,128)(2,1)}, bf16[2,8,72,2048]{3,2,1,0:T(8,128)(2,1)S(1)}, u32[]{:S(2)}) copy-start(bf16[2,8,72,2048]{3,2,1,0:T(8,128)(2,1)S(1)} %copy.27) | copy-start | bytes 14155780
  111.3 3.6 %copy-start.3 = (bf16[2,2048,384]{2,1,0:T(8,128)(2,1)S(1)}, bf16[2,2048,384]{2,1,0:T(8,128)(2,1)}, u32[]{:S(2)}) copy-start(bf16[2,2048,384]{2,1,0:T(8,128)(2,1)} %param.12) | copy-start | bytes 9437188
  111.3 6.2 %slice-start = ((s8[4718592]{0:T(1024)(128)(4,1)}), s8[4194304]{0:T(1024)(128)(4,1)S(1)}, s32[]{:S(2)}) async-start(s8[4718592]{0:T(1024)(128)(4,1)} %bitcast.66), calls=%async_computation.5 | async-start | bytes 8388608
  114.9 2.6 %slice-start.1 = ((s8[4718592]{0:T(1024)(128)(4,1)}), s8[524288]{0:T(1024)(128)(4,1)S(1)}, s32[]{:S(2)}) async-start(s8[4718592]{0:T(1024)(128)(4,1)} %bitcast.66), calls=%async_computation.6 | async-start | bytes 1048576
  114.9 2.6 %copy-start.9 = (bf16[2,384,2048]{2,1,0:T(8,128)(2,1)S(1)}, bf16[2,384,2048]{2,1,0:T(8,128)(2,1)}, u32[]{:S(2)}) copy-start(bf16[2,384,2048]{2,1,0:T(8,128)(2,1)} %param.13) | copy-start | bytes 9437188
  122.2 2.8 %copy-start.4 = (bf16[2,576,384]{2,1,0:T(8,128)(2,1)}, bf16[2,576,384]{2,1,0:T(8,128)(2,1)S(1)}, u32[]{:S(2)}) copy-start(bf16[2,576,384]{2,1,0:T(8,128)(2,1)S(1)} %get-tuple-element.6) | copy-start | bytes 2654212
  132.6 1.2 copy-start.7
  132.6 7.1 %copy-start.5 = (bf16[2,576,384]{2,1,0:T(8,128)(2,1)S(1)}, bf16[2,576,384]{2,1,0:T(8,128)(2,1)}, u32[]{:S(2)}) copy-start(bf16[2,576,384]{2,1,0:T(8,128)(2,1)} %copy-done.4) | copy-start | bytes 2654212
  138.3 6.5 %copy-start.10 = (bf16[2,576,384]{2,1,0:T(8,128)(2,1)S(1)}, bf16[2,576,384]{2,1,0:T(8,128)(2,1)}, u32[]{:S(2)}) copy-start(bf16[2,576,384]{2,1,0:T(8,128)(2,1)} %get-tuple-element.7) | copy-start | bytes 2654212
  138.3 37.5 %collective-permute-start.1 = (bf16[2,1024,384]{2,1,0:T(8,128)(2,1)}, bf16[2,1024,384]{2,1,0:T(8,128)(2,1)}, u32[]{:S(2)}, u32[]{:S(2)}) collective-permute-start(bf16[2,1024,384]{2,1,0:T(8,128)(2,1)} %fusion.26), channel_id=1, source_target_pairs={{0,1},{1,0},{2,3},{3,2},{4,5},{5,4},{6,7},{7,6},{8,9},{9,8},{10,11... | collective-permute-start | bytes 4718600 | tf_op jit(solution)/shard_map/ppermute | solution.py:23
  144.3 65.3 %collective-permute-start = (bf16[2,1024,384]{2,1,0:T(8,128)(2,1)}, bf16[2,1024,384]{2,1,0:T(8,128)(2,1)}, u32[]{:S(2)}, u32[]{:S(2)}) collective-permute-start(bf16[2,1024,384]{2,1,0:T(8,128)(2,1)} %fusion.23), channel_id=1, source_target_pairs={{0,1},{1,0},{2,3},{3,2},{4,5},{5,4},{6,7},{7,6},{8,9},{9,8},{10,11... | collective-permute-start | bytes 4718600 | tf_op jit(solution)/shard_map/ppermute | solution.py:23
  144.8 15.6 %copy-start.8 = (s32[128,8]{0,1:T(8,128)S(1)}, s32[128,8]{0,1:T(8,128)}, u32[]{:S(2)}) copy-start(s32[128,8]{0,1:T(8,128)} %param.9) | copy-start | bytes 12292
  149.1 93.4 %collective-permute-start.2 = (bf16[2,384,1024]{2,1,0:T(8,128)(2,1)}, bf16[2,384,1024]{2,1,0:T(8,128)(2,1)}, u32[]{:S(2)}, u32[]{:S(2)}) collective-permute-start(bf16[2,384,1024]{2,1,0:T(8,128)(2,1)} %fusion.32), channel_id=1, source_target_pairs={{0,1},{1,0},{2,3},{3,2},{4,5},{5,4},{6,7},{7,6},{8,9},{9,8},{10,11... | collective-permute-start | bytes 4718600 | tf_op jit(solution)/shard_map/ppermute | solution.py:23
  151.5 8.9 %all-to-all-start = ((bf16[8,2,128]{2,1,0:T(2,128)(2,1)}), bf16[8,2,128]{2,1,0:T(2,128)(2,1)S(1)}, u32[]{:S(2)}, u32[]{:S(2)}) async-start(bf16[8,2,128]{2,1,0:T(2,128)(2,1)} %convert_element_type.130), calls=%async_computation.1 | async-start | bytes 8192 | tf_op jit(solution)/shard_map/all_to_all | solution.py:85
  161.0 48.5 %copy-start.6 = (bf16[2,576,384]{2,1,0:T(8,128)(2,1)S(1)}, bf16[2,576,384]{2,1,0:T(8,128)(2,1)}, u32[]{:S(2)}) copy-start(bf16[2,576,384]{2,1,0:T(8,128)(2,1)} %copy-done.4) | copy-start | bytes 2654212
  180.9 61.7 %copy-start.11 = (bf16[2,576,384]{2,1,0:T(8,128)(2,1)S(1)}, bf16[2,576,384]{2,1,0:T(8,128)(2,1)}, u32[]{:S(2)}) copy-start(bf16[2,576,384]{2,1,0:T(8,128)(2,1)} %get-tuple-element.7) | copy-start | bytes 2654212
  209.5 37.7 %copy-start.1 = (bf16[2,2048,384]{2,1,0:T(8,128)(2,1)S(1)}, bf16[2,2048,384]{2,1,0:T(8,128)(2,1)}, u32[]{:S(2)}) copy-start(bf16[2,2048,384]{2,1,0:T(8,128)(2,1)} %param.11) | copy-start | bytes 9437188
Sparse Core Ops, SparseCore 0:
  9.6 49.8 all-gather.5
  61.1 45.9 all-gather.7
  132.7 48.7 reduce-scatter.1

commit v3 on v2

--- a/solution.py
+++ b/solution.py
@@ -1,10 +1,109 @@
+import functools
+
 import jax
 import jax.numpy as jnp
 from jax import lax
+from jax.experimental import pallas as pl
+from jax.experimental.pallas import tpu as pltpu
 from jax.sharding import PartitionSpec as P
 
 BF = jnp.bfloat16
 F32 = jnp.float32
+
+
+def gather_kernel(chips, count, *refs):
+    ins, outs = refs[:count], refs[count : 2 * count]
+    local_sem, up_sem, down_sem, side_sem, line_recv, side_recv = refs[2 * count :]
+    me = lax.axis_index("expert")
+    chip, core = me // 2, me % 2
+    side = chip * 2 + 1 - core
+    above, below = me + 2, me - 2
+    has_above, has_below = chip < chips - 1, chip > 0
+
+    barrier = pltpu.get_barrier_semaphore()
+    pl.semaphore_signal(barrier, inc=1, device_id={"expert": side}, device_id_type=pl.DeviceIdType.MESH)
+
+    @pl.when(has_above)
+    def _():
+        pl.semaphore_signal(barrier, inc=1, device_id={"expert": above}, device_id_type=pl.DeviceIdType.MESH)
+
+    @pl.when(has_below)
+    def _():
+        pl.semaphore_signal(barrier, inc=1, device_id={"expert": below}, device_id_type=pl.DeviceIdType.MESH)
+
+    peers = 1 + jnp.where(has_above, 1, 0) + jnp.where(has_below, 1, 0)
+    pl.semaphore_wait(barrier, peers)
+
+    def copy(which, src, origin, sems, recvs, target, from_core):
+        return pltpu.make_async_remote_copy(
+            src_ref=src,
+            dst_ref=outs[which].at[origin * 2 + from_core],
+            send_sem=sems.at[origin, which],
+            recv_sem=recvs.at[origin, which],
+            device_id={"expert": target},
+            device_id_type=pl.DeviceIdType.MESH,
+        )
+
+    def up(which, src, origin):
+        return copy(which, src, origin, up_sem, line_recv, above, core)
+
+    def down(which, src, origin):
+        return copy(which, src, origin, down_sem, line_recv, below, core)
+
+    def across(which, src, origin):
+        return copy(which, src, origin, side_sem, side_recv, side, core)
+
+    def own(which):
+        return pltpu.make_async_copy(ins[which], outs[which].at[me], local_sem.at[which])
+
+    for which in range(count):
+        pl.when(has_above)(lambda w=which: up(w, ins[w], chip).start())
+        pl.when(has_below)(lambda w=which: down(w, ins[w], chip).start())
+    for which in range(count):
+        across(which, ins[which], chip).start()
+        own(which).start()
+
+    for far in range(1, chips):
+        for which in range(count):
+
+            @pl.when(chip - far >= 0)
+            def _(which=which, origin=chip - far):
+                block = outs[which].at[origin * 2 + core]
+                up(which, block, origin).wait_recv()
+                pl.when(has_above)(lambda: up(which, block, origin).start())
+                across(which, block, origin).start()
+
+            @pl.when(chip + far < chips)
+            def _(which=which, origin=chip + far):
+                block = outs[which].at[origin * 2 + core]
+                down(which, block, origin).wait_recv()
+                pl.when(has_below)(lambda: down(which, block, origin).start())
+                across(which, block, origin).start()
+
+    for which in range(count):
+        own(which).wait()
+        for origin in range(chips):
+            block = outs[which].at[origin * 2 + core]
+            across(which, block, origin).wait_send()
+            copy(which, block, origin, side_sem, side_recv, side, 1 - core).wait_recv()
+            pl.when(has_above & (origin <= chip))(lambda w=which, b=block, o=origin: up(w, b, o).wait_send())
+            pl.when(has_below & (origin >= chip))(lambda w=which, b=block, o=origin: down(w, b, o).wait_send())
+
+
+def gather(*arrays):
+    n = lax.axis_size("expert")
+    chips, count = n // 2, len(arrays)
+    size = sum(a.size * a.dtype.itemsize for a in arrays)
+    return pl.pallas_call(
+        functools.partial(gather_kernel, chips, count),
+        out_shape=[jax.ShapeDtypeStruct((n,) + a.shape, a.dtype) for a in arrays],
+        in_specs=[pl.BlockSpec(memory_space=pl.ANY)] * count,
+        out_specs=[pl.BlockSpec(memory_space=pl.ANY)] * count,
+        scratch_shapes=[pltpu.SemaphoreType.DMA((count,))] + [pltpu.SemaphoreType.DMA((chips, count))] * 5,
+        compiler_params=pltpu.CompilerParams(collective_id=0, has_side_effects=True),
+        cost_estimate=pl.CostEstimate(flops=0, bytes_accessed=2 * n * size, transcendentals=0),
+        name="gather_line",
+    )(*arrays)
 
 
 def halves(rows):
@@ -38,9 +137,8 @@
     hit = routes[:, :, None] == names[None, None, :]
     gate_map = jnp.sum(jnp.where(hit, gates[:, :, None].astype(F32), 0.0), axis=1).astype(BF)
 
-    all_map = lax.all_gather(gate_map, "expert", axis=0)
-    all_x = lax.all_gather(tokens, "expert", axis=0)
-    all_dy = lax.all_gather(out_grads, "expert", axis=0)
+    pad = -experts % 128
+    all_x, all_dy, all_map = gather(tokens, out_grads, jnp.pad(gate_map, ((0, 0), (0, pad))))
 
     mine = lax.dynamic_slice_in_dim(all_map, me * local, local, axis=2).transpose(2, 0, 1)
     used = mine > 0

time: 254 us -> 243 us (0.957)
  waiting for transfers between devices: 154 us -> 76.5 us
  Pallas kernels: 0 us -> 77 us
  blocking collectives: 14.4 us -> 0 us
  local copies, waits for them, and re-layouts: 5.45 us -> 8.95 us
    pallas_call x0 -> x1, Pallas kernels: none -> 77 us  [gather(): pl.pallas_call(functools.partial(gather_kernel, chips, count), out_shape=...]
    all_gather x2 -> x0, waiting for transfers between devices: 75.9 us -> none  [the longest x1 41.5 us: per_device(): all_x = lax.all_gather(tokens, 'expert', axis=0)]
    all_gather x1 -> x0, blocking collectives: 14.4 us -> none  [per_device(): all_map = lax.all_gather(gate_map, 'expert', axis=0)]
    unnamed x29 -> x28, local copies, waits for them, and re-layouts: 2.13 us -> 4.86 us
  transfers between devices with their start and end apart: 7 -> 5, of which waited for: 6 -> 4; matrix products, arithmetic and copies ran while one was open for 15% -> 12% of each run, Pallas kernels for 0% -> 0%
where the time goes in v3:
time: 243 us; the launch traced here: 242 us
  Pallas kernels  77 us (32%)
  waiting for transfers between devices  76.5 us (31%)
  matrix products  54.1 us (22%)
  between operations  14.3 us (6%)
  local copies, waits for them, and re-layouts  8.95 us (4%)
  starting transfers between devices  7.42 us (3%)
  other arithmetic  3.91 us (2%)
    pallas_call x1, Pallas kernels, gather(): pl.pallas_call(functools.partial(gather_kernel, chips, count), out_shape=...  77 us
    ppermute x3, waiting for transfers between devices, replica_sum(): other = lax.ppermute(grad(give).astype(BF), 'dp', [(0, 1), (1, 0)])  70.9 us
    dot_general x2, matrix products, per_device(): jnp.einsum('lcd,lcf->ldf', d, grad_gate, preferred_element_type=F32)  9.67 us
    dot_general x2, matrix products, per_device(): jnp.einsum('lcd,lcf->ldf', d, grad_up, preferred_element_type=F32)  9.54 us
    dot_general x2, matrix products, per_device(): jnp.einsum('lcf,lcd->lfd', gated_hidden, d, preferred_element_type=F32)  9 us
    all_to_all x1, waiting for transfers between devices, per_device(): lax.all_to_all(back_route, 'expert', split_axis=0, concat_axis=0, tiled=T...  5.62 us
  transfers between devices with their start and end apart: 5, of which 4 were waited for; matrix products, arithmetic and copies ran while one was open for 12% of the time, Pallas kernels for 0%

profile of v3, /device:TPU:0, one launch (start us, length us, event | category | flops | bytes accessed | tf_op | source)
XLA Modules:
  0.0 242.1 jit_solution(4822952233858124625)
XLA Ops:
  7.2 0.8 convert_element_type.108
  8.1 0.8 select_reduce_fusion.1
  9.6 77.0 %gather_line.1 = (bf16[8,128,2048]{2,1,0:T(8,128)(2,1)}, bf16[8,128,2048]{2,1,0:T(8,128)(2,1)}, bf16[8,128,128]{2,1,0:T(8,128)(2,1)}) custom-call(bf16[128,2048]{1,0:T(8,128)(2,1)} %refs_0_.1, bf16[128,2048]{1,0:T(8,128)(2,1)} %refs_1_.1, bf16[128,128]{1,0:T(8,128)(2,1)} %pad.4.refs_2_), custom_call_target="tpu_custom_call" | custom-call | bytes 17301504 | tf_op jit(solution)/shard_map/gather_line/pallas_call | solution.py:97
  86.6 1.1 bitcast_compare_fusion
  87.7 1.1 dynamic-slice_bitcast_fusion
  90.1 3.6 %convert_bitcast_fusion.1 = bf16[2,8,72,2048]{3,2,0,1:T(8,128)(2,1)S(1)} fusion(bf16[8,128,2048]{2,1,0:T(8,128)(2,1)} %get-tuple-element.9, s32[2,8,128]{2,0,1:T(2,128)S(1)} %copy.36, pred[2,8,128]{2,0,1:T(4,128)(4,1)S(1)} %copy.37), kind=kOutput, calls=%fused_computation.5 | convolution fusion | flops 606633984 | bytes 8923136 | tf_op jit(solution)/shard_map/lsct,std->lscd/dot_general | solution.py:160
  93.6 0.7 copy.38
  94.4 2.7 %copy-done.4 = bf16[8,128,2048]{2,1,0:T(8,128)(2,1)S(1)} copy-done((bf16[8,128,2048]{2,1,0:T(8,128)(2,1)S(1)}, bf16[8,128,2048]{2,1,0:T(8,128)(2,1)}, u32[]{:S(2)}) %copy-start.4) | copy-done | bytes 4194328
  97.1 1.4 convert_bitcast_fusion
  98.5 0.7 copy.39
  99.2 2.6 %fusion.75 = f32[2,576,384]{2,1,0:T(8,128)S(1)} fusion(bf16[2,576,2048]{2,1,0:T(8,128)(2,1)S(1)} %bitcast.64, bf16[2,2048,384]{2,1,0:T(8,128)(2,1)S(1)} %copy-done), kind=kOutput, calls=%fused_computation.68 | convolution fusion | flops 1811939328 | bytes 9633792 | tf_op jit(solution)/shard_map/lcd,ldf->lcf/dot_general | solution.py:154
  101.9 0.9 copy-done.5
  102.8 2.6 %fusion.74 = f32[2,576,384]{2,1,0:T(8,128)S(1)} fusion(bf16[2,576,2048]{2,1,0:T(8,128)(2,1)S(1)} %bitcast.65, bf16[2,2048,384]{2,1,0:T(8,128)(2,1)S(1)} %copy-done.5), kind=kOutput, calls=%fused_computation.67 | convolution fusion | flops 1811939328 | bytes 9633792 | tf_op jit(solution)/shard_map/lcd,ldf->lcf/dot_general | solution.py:155
  105.4 4.7 %multiply_reduce_fusion = (bf16[2,576]{1,0:T(2,128)(2,1)S(1)}, bf16[2,576,384]{2,1,0:T(8,128)(2,1)S(1)}, bf16[2,576,384]{2,1,0:T(8,128)(2,1)}, bf16[2,576,384]{2,1,0:T(8,128)(2,1)}) fusion(f32[2,576,384]{2,1,0:T(8,128)S(1)} %fusion.74, f32[2,576,384]{2,1,0:T(8,128)S(1)} %fusion.75, f32[2,576]{1,0:T(2,128)S(1)} %mul.52, ...), kind=kOutput, calls=%fused_computation.26 | convolution fusion | flops 1820343168 | bytes 14064384 | tf_op jit(solution)/shard_map/lcd,lfd->lcf/dot_general | solution.py:164
  110.1 2.8 %fusion.76 = f32[2,576,2048]{2,1,0:T(8,128)S(1)} fusion(bf16[2,576,384]{2,1,0:T(8,128)(2,1)S(1)} %get-tuple-element.12, bf16[2,2048,384]{2,1,0:T(8,128)(2,1)S(1)} %copy-done), kind=kOutput, calls=%fused_computation.69 | convolution fusion | flops 1811939328 | bytes 13467648 | tf_op jit(solution)/shard_map/lcf,ldf->lcd/dot_general | solution.py:174
  113.0 4.1 %add_convert_fusion = bf16[2,576,2048]{2,1,0:T(8,128)(2,1)S(1)} fusion(f32[2,576,2048]{2,1,0:T(8,128)S(1)} %fusion.76, bf16[2,576,384]{2,1,0:T(8,128)(2,1)} %get-tuple-element.14, bf16[2,2048,384]{2,1,0:T(8,128)(2,1)S(1)} %copy-done.5), kind=kOutput, calls=%fused_computation | convolution fusion | flops 1816657920 | bytes 18186240 | tf_op jit(solution)/shard_map/lcf,ldf->lcd/dot_general | solution.py:175
  117.1 3.4 %bitcast_convert_fusion = bf16[8,128,2048]{2,1,0:T(8,128)(2,1)} fusion(bf16[2,8,72,2048]{3,2,1,0:T(8,128)(2,1)S(1)} %bitcast.60, s32[2,8,128]{2,0,1:T(2,128)S(1)} %copy.36, pred[2,8,128]{2,0,1:T(4,128)(4,1)S(1)} %copy.37), kind=kOutput, calls=%fused_computation.1 | convolution fusion | flops 606371840 | bytes 8923136 | tf_op jit(solution)/shard_map/lsct,lscd->std/dot_general | solution.py:177
  120.5 1.1 copy-done.9
  121.7 4.5 %fusion.34 = bf16[2,1024,384]{2,1,0:T(8,128)(2,1)} fusion(bf16[2,576,384]{2,1,0:T(8,128)(2,1)S(1)} %copy-done.9, bf16[2,576,2048]{2,1,0:T(8,128)(2,1)} %bitcast.66, s32[]{:T(128)S(6)} %select_n.28), kind=kOutput, calls=%fused_computation.34 | convolution fusion | flops 906756096 | bytes 4816900 | tf_op jit(solution)/shard_map/lcd,lcf->ldf/dot_general | solution.py:171
  126.2 1.5 collective-permute-start.1
  127.7 4.5 %fusion.31 = bf16[2,1024,384]{2,1,0:T(8,128)(2,1)} fusion(bf16[2,576,384]{2,1,0:T(8,128)(2,1)S(1)} %copy-done.7, bf16[2,576,2048]{2,1,0:T(8,128)(2,1)} %bitcast.67, s32[]{:T(128)S(6)} %select_n.28), kind=kOutput, calls=%fused_computation.33 | convolution fusion | flops 906756096 | bytes 4816900 | tf_op jit(solution)/shard_map/lcd,lcf->ldf/dot_general | solution.py:170
  132.2 0.7 collective-permute-start
  132.9 4.3 %fusion.40 = bf16[2,384,1024]{2,1,0:T(8,128)(2,1)} fusion(bf16[2,576,384]{2,1,0:T(8,128)(2,1)S(1)} %copy-done.12, bf16[2,576,2048]{2,1,0:T(8,128)(2,1)} %bitcast.62, s32[]{:T(128)S(6)} %select_n.28), kind=kOutput, calls=%fused_computation.36 | convolution fusion | flops 906756096 | bytes 4816900 | tf_op jit(solution)/shard_map/lcf,lcd->lfd/dot_general | solution.py:163
  137.2 1.4 collective-permute-start.2
  139.4 3.9 %all-to-all-start = ((bf16[8,2,128]{2,1,0:T(2,128)(2,1)}), bf16[8,2,128]{2,1,0:T(2,128)(2,1)S(1)}, u32[]{:S(2)}, u32[]{:S(2)}) async-start(bf16[8,2,128]{2,1,0:T(2,128)(2,1)} %convert_element_type.121), calls=%async_computation.1 | async-start | bytes 8192 | tf_op jit(solution)/shard_map/all_to_all | solution.py:183
  143.3 5.6 %all-to-all-done = bf16[8,2,128]{2,1,0:T(2,128)(2,1)S(1)} async-done(((bf16[8,2,128]{2,1,0:T(2,128)(2,1)}), bf16[8,2,128]{2,1,0:T(2,128)(2,1)S(1)}, u32[]{:S(2)}, u32[]{:S(2)}) %all-to-all-start) | async-done | bytes 4128 | tf_op jit(solution)/shard_map/all_to_all | solution.py:183
  149.5 14.2 %collective-permute-done.1 = bf16[2,1024,384]{2,1,0:T(8,128)(2,1)} collective-permute-done((bf16[2,1024,384]{2,1,0:T(8,128)(2,1)}, bf16[2,1024,384]{2,1,0:T(8,128)(2,1)}, u32[]{:S(2)}, u32[]{:S(2)}) %collective-permute-start.1) | collective-permute-done | bytes 1572896 | tf_op jit(solution)/shard_map/ppermute | solution.py:122
  163.7 5.0 %add_convert_fusion.2 = bf16[2,1024,384]{2,1,0:T(8,128)(2,1)} fusion(bf16[2,1024,384]{2,1,0:T(8,128)(2,1)} %collective-permute-done.1, bf16[2,576,384]{2,1,0:T(8,128)(2,1)S(1)} %copy-done.9, bf16[2,576,2048]{2,1,0:T(8,128)(2,1)} %bitcast.68, s32[]{:T(128)S(6)} %select_n.27), kind=kOutput, calls=%fused_computation.11 | convolution fusion | flops 909901824 | bytes 6389764 | tf_op jit(solution)/shard_map/lcd,lcf->ldf/dot_general | solution.py:171
  168.7 28.7 %collective-permute-done = bf16[2,1024,384]{2,1,0:T(8,128)(2,1)} collective-permute-done((bf16[2,1024,384]{2,1,0:T(8,128)(2,1)}, bf16[2,1024,384]{2,1,0:T(8,128)(2,1)}, u32[]{:S(2)}, u32[]{:S(2)}) %collective-permute-start) | collective-permute-done | bytes 1572896 | tf_op jit(solution)/shard_map/ppermute | solution.py:122
  197.4 5.2 %add_convert_fusion.3 = bf16[2,1024,384]{2,1,0:T(8,128)(2,1)} fusion(bf16[2,1024,384]{2,1,0:T(8,128)(2,1)} %collective-permute-done, bf16[2,576,384]{2,1,0:T(8,128)(2,1)S(1)} %copy-done.8, bf16[2,576,2048]{2,1,0:T(8,128)(2,1)} %bitcast.69, s32[]{:T(128)S(6)} %select_n.27), kind=kOutput, calls=%fused_computation.12 | convolution fusion | flops 909901824 | bytes 6389764 | tf_op jit(solution)/shard_map/lcd,lcf->ldf/dot_general | solution.py:170
  202.6 28.0 %collective-permute-done.2 = bf16[2,384,1024]{2,1,0:T(8,128)(2,1)} collective-permute-done((bf16[2,384,1024]{2,1,0:T(8,128)(2,1)}, bf16[2,384,1024]{2,1,0:T(8,128)(2,1)}, u32[]{:S(2)}, u32[]{:S(2)}) %collective-permute-start.2) | collective-permute-done | bytes 1572896 | tf_op jit(solution)/shard_map/ppermute | solution.py:122
  230.6 4.7 %add_convert_fusion.1 = bf16[2,384,1024]{2,1,0:T(8,128)(2,1)} fusion(bf16[2,384,1024]{2,1,0:T(8,128)(2,1)} %collective-permute-done.2, bf16[2,576,384]{2,1,0:T(8,128)(2,1)S(1)} %copy-done.13, bf16[2,576,2048]{2,1,0:T(8,128)(2,1)} %bitcast.63, s32[]{:T(128)S(6)} %select_n.27), kind=kOutput, calls=%fused_computation.10 | convolution fusion | flops 909901824 | bytes 6389764 | tf_op jit(solution)/shard_map/lcf,lcd->lfd/dot_general | solution.py:163
  (43 shorter events, 3.6 us)
Async XLA Ops:
  7.2 92.0 %copy-start = (bf16[2,2048,384]{2,1,0:T(8,128)(2,1)S(1)}, bf16[2,2048,384]{2,1,0:T(8,128)(2,1)}, u32[]{:S(2)}) copy-start(bf16[2,2048,384]{2,1,0:T(8,128)(2,1)} %param.11) | copy-start | bytes 9437188
  7.2 228.1 %reduce-scatter.2.cloned.1.call-start = ((), (), s32[]{:S(2)}) async-start(), calls=%async_computation.2 | async-start | bytes 4718592 | tf_op jit(solution)/shard_map/reduce_scatter | solution.py:178
  93.6 3.5 %copy-start.4 = (bf16[8,128,2048]{2,1,0:T(8,128)(2,1)S(1)}, bf16[8,128,2048]{2,1,0:T(8,128)(2,1)}, u32[]{:S(2)}) copy-start(bf16[8,128,2048]{2,1,0:T(8,128)(2,1)} %get-tuple-element.10) | copy-start | bytes 12582916
  94.3 11.1 %copy-start.2 = (bf16[2,8,72,2048]{3,2,1,0:T(8,128)(2,1)}, bf16[2,8,72,2048]{3,2,1,0:T(8,128)(2,1)S(1)}, u32[]{:S(2)}) copy-start(bf16[2,8,72,2048]{3,2,1,0:T(8,128)(2,1)S(1)} %copy.38) | copy-start | bytes 14155780
  99.2 2.7 %copy-start.3 = (bf16[2,8,72,2048]{3,2,1,0:T(8,128)(2,1)}, bf16[2,8,72,2048]{3,2,1,0:T(8,128)(2,1)S(1)}, u32[]{:S(2)}) copy-start(bf16[2,8,72,2048]{3,2,1,0:T(8,128)(2,1)S(1)} %copy.39) | copy-start | bytes 14155780
  99.2 3.6 %copy-start.5 = (bf16[2,2048,384]{2,1,0:T(8,128)(2,1)S(1)}, bf16[2,2048,384]{2,1,0:T(8,128)(2,1)}, u32[]{:S(2)}) copy-start(bf16[2,2048,384]{2,1,0:T(8,128)(2,1)} %param.12) | copy-start | bytes 9437188
  102.8 2.6 %copy-start.11 = (bf16[2,384,2048]{2,1,0:T(8,128)(2,1)S(1)}, bf16[2,384,2048]{2,1,0:T(8,128)(2,1)}, u32[]{:S(2)}) copy-start(bf16[2,384,2048]{2,1,0:T(8,128)(2,1)} %param.13) | copy-start | bytes 9437188
  110.1 2.9 %copy-start.6 = (bf16[2,576,384]{2,1,0:T(8,128)(2,1)}, bf16[2,576,384]{2,1,0:T(8,128)(2,1)S(1)}, u32[]{:S(2)}) copy-start(bf16[2,576,384]{2,1,0:T(8,128)(2,1)S(1)} %get-tuple-element.12) | copy-start | bytes 2654212
  120.5 1.2 copy-start.9
  120.5 7.2 %copy-start.7 = (bf16[2,576,384]{2,1,0:T(8,128)(2,1)S(1)}, bf16[2,576,384]{2,1,0:T(8,128)(2,1)}, u32[]{:S(2)}) copy-start(bf16[2,576,384]{2,1,0:T(8,128)(2,1)} %copy-done.6) | copy-start | bytes 2654212
  126.2 6.7 %copy-start.12 = (bf16[2,576,384]{2,1,0:T(8,128)(2,1)S(1)}, bf16[2,576,384]{2,1,0:T(8,128)(2,1)}, u32[]{:S(2)}) copy-start(bf16[2,576,384]{2,1,0:T(8,128)(2,1)} %get-tuple-element.13) | copy-start | bytes 2654212
  126.2 37.5 %collective-permute-start.1 = (bf16[2,1024,384]{2,1,0:T(8,128)(2,1)}, bf16[2,1024,384]{2,1,0:T(8,128)(2,1)}, u32[]{:S(2)}, u32[]{:S(2)}) collective-permute-start(bf16[2,1024,384]{2,1,0:T(8,128)(2,1)} %fusion.34), channel_id=1, source_target_pairs={{0,1},{1,0},{2,3},{3,2},{4,5},{5,4},{6,7},{7,6},{8,9},{9,8},{10,11... | collective-permute-start | bytes 4718600 | tf_op jit(solution)/shard_map/ppermute | solution.py:122
  132.2 65.2 %collective-permute-start = (bf16[2,1024,384]{2,1,0:T(8,128)(2,1)}, bf16[2,1024,384]{2,1,0:T(8,128)(2,1)}, u32[]{:S(2)}, u32[]{:S(2)}) collective-permute-start(bf16[2,1024,384]{2,1,0:T(8,128)(2,1)} %fusion.31), channel_id=1, source_target_pairs={{0,1},{1,0},{2,3},{3,2},{4,5},{5,4},{6,7},{7,6},{8,9},{9,8},{10,11... | collective-permute-start | bytes 4718600 | tf_op jit(solution)/shard_map/ppermute | solution.py:122
  132.9 16.1 %copy-start.10 = (s32[128,8]{0,1:T(8,128)S(1)}, s32[128,8]{0,1:T(8,128)}, u32[]{:S(2)}) copy-start(s32[128,8]{0,1:T(8,128)} %param.9) | copy-start | bytes 12292
  137.2 93.4 %collective-permute-start.2 = (bf16[2,384,1024]{2,1,0:T(8,128)(2,1)}, bf16[2,384,1024]{2,1,0:T(8,128)(2,1)}, u32[]{:S(2)}, u32[]{:S(2)}) collective-permute-start(bf16[2,384,1024]{2,1,0:T(8,128)(2,1)} %fusion.40), channel_id=1, source_target_pairs={{0,1},{1,0},{2,3},{3,2},{4,5},{5,4},{6,7},{7,6},{8,9},{9,8},{10,11... | collective-permute-start | bytes 4718600 | tf_op jit(solution)/shard_map/ppermute | solution.py:122
  139.4 9.5 %all-to-all-start = ((bf16[8,2,128]{2,1,0:T(2,128)(2,1)}), bf16[8,2,128]{2,1,0:T(2,128)(2,1)S(1)}, u32[]{:S(2)}, u32[]{:S(2)}) async-start(bf16[8,2,128]{2,1,0:T(2,128)(2,1)} %convert_element_type.121), calls=%async_computation.1 | async-start | bytes 8192 | tf_op jit(solution)/shard_map/all_to_all | solution.py:183
  149.5 47.9 %copy-start.8 = (bf16[2,576,384]{2,1,0:T(8,128)(2,1)S(1)}, bf16[2,576,384]{2,1,0:T(8,128)(2,1)}, u32[]{:S(2)}) copy-start(bf16[2,576,384]{2,1,0:T(8,128)(2,1)} %copy-done.6) | copy-start | bytes 2654212
  168.7 61.8 %copy-start.13 = (bf16[2,576,384]{2,1,0:T(8,128)(2,1)S(1)}, bf16[2,576,384]{2,1,0:T(8,128)(2,1)}, u32[]{:S(2)}) copy-start(bf16[2,576,384]{2,1,0:T(8,128)(2,1)} %get-tuple-element.13) | copy-start | bytes 2654212
  197.4 37.9 %copy-start.1 = (bf16[2,2048,384]{2,1,0:T(8,128)(2,1)S(1)}, bf16[2,2048,384]{2,1,0:T(8,128)(2,1)}, u32[]{:S(2)}) copy-start(bf16[2,2048,384]{2,1,0:T(8,128)(2,1)} %param.11) | copy-start | bytes 9437188
Sparse Core Ops, SparseCore 0:
  120.6 50.1 reduce-scatter.1

commit v4 on v3

--- a/solution.py
+++ b/solution.py
@@ -106,6 +106,19 @@
     )(*arrays)
 
 
+SWAP = [(0, 1), (1, 0)]
+
+
+def picks(gate, cap):
+    used = gate > 0
+    tok_rows = gate.shape[-1]
+    tri = jnp.triu(jnp.ones((tok_rows, tok_rows), BF))
+    place = jnp.dot(used.astype(BF).reshape(-1, tok_rows), tri, preferred_element_type=F32)
+    place = place.astype(jnp.int32).reshape(used.shape) - 1
+    slots = jnp.arange(cap, dtype=jnp.int32)[None, None, :, None]
+    return ((place[:, :, None, :] == slots) & used[:, :, None, :]).astype(BF)
+
+
 def halves(rows):
     if lax.axis_size("dp") != 2:
         return rows, rows
@@ -119,7 +132,7 @@
 def replica_sum(grad, give, keep, dim):
     if lax.axis_size("dp") != 2:
         return lax.psum_scatter(grad(keep).astype(BF), "dp", scatter_dimension=dim, tiled=True)
-    other = lax.ppermute(grad(give).astype(BF), "dp", [(0, 1), (1, 0)])
+    other = lax.ppermute(grad(give).astype(BF), "dp", SWAP)
     own = grad(keep).astype(BF)
     return (own.astype(F32) + other.astype(F32)).astype(BF)
 
@@ -137,16 +150,20 @@
     hit = routes[:, :, None] == names[None, None, :]
     gate_map = jnp.sum(jnp.where(hit, gates[:, :, None].astype(F32), 0.0), axis=1).astype(BF)
 
+    paired = lax.axis_size("dp") == 2
+    if paired:
+        other_x = lax.ppermute(halves(tokens)[0], "dp", SWAP)
     pad = -experts % 128
     all_x, all_dy, all_map = gather(tokens, out_grads, jnp.pad(gate_map, ((0, 0), (0, pad))))
 
     mine = lax.dynamic_slice_in_dim(all_map, me * local, local, axis=2).transpose(2, 0, 1)
-    used = mine > 0
-    tri = jnp.triu(jnp.ones((tok_rows, tok_rows), BF))
-    place = jnp.dot(used.astype(BF).reshape(-1, tok_rows), tri, preferred_element_type=F32)
-    place = place.astype(jnp.int32).reshape(used.shape) - 1
-    pick = (place[:, :, None, :] == jnp.arange(cap, dtype=jnp.int32)[None, None, :, None]) & used[:, :, None, :]
-    pick = pick.astype(BF)
+    pick = picks(mine, cap)
+    if paired:
+        other_pick = picks(lax.ppermute(mine, "dp", SWAP), cap)
+        other_x, all_x = lax.optimization_barrier((other_x, all_x))
+        other_x = lax.all_gather(other_x, "expert", axis=0)
+        other_rows = jnp.einsum("lsct,std->lscd", other_pick, other_x, preferred_element_type=F32).astype(BF)
+        other_rows = other_rows.reshape(local, groups * cap, width // 2)
     gate_col = jnp.einsum("lsct,lst->lsc", pick, mine, preferred_element_type=F32)
     gate_col = gate_col.reshape(local, -1, 1)
     rows_x = jnp.einsum("lsct,std->lscd", pick, all_x, preferred_element_type=F32).astype(BF)
@@ -159,16 +176,30 @@
     gated_hidden = (gate_col * hidden).astype(BF)
     rows_dy = jnp.einsum("lsct,std->lscd", pick, all_dy, preferred_element_type=F32).astype(BF)
     rows_dy = rows_dy.reshape(local, groups * cap, width)
-    give_dy, keep_dy = halves(rows_dy)
-    down_sum = replica_sum(lambda d: jnp.einsum("lcf,lcd->lfd", gated_hidden, d, preferred_element_type=F32), give_dy, keep_dy, 2)
     back_raw = jnp.einsum("lcd,lfd->lcf", rows_dy, down_weight, preferred_element_type=F32)
     route_grad = jnp.sum(hidden * back_raw, axis=-1).astype(BF)
     back = gate_col * back_raw
     grad_gate = (back * pre_up * sig * (1.0 + pre_gate * (1.0 - sig))).astype(BF)
     grad_up = (back * act).astype(BF)
+    if paired:
+        gated_hidden, grad_gate, grad_up = lax.optimization_barrier((gated_hidden, grad_gate, grad_up))
+        other_gate = lax.ppermute(grad_gate, "dp", SWAP)
+        other_up = lax.ppermute(grad_up, "dp", SWAP)
+    give_dy, keep_dy = halves(rows_dy)
+    down_sum = replica_sum(lambda d: jnp.einsum("lcf,lcd->lfd", gated_hidden, d, preferred_element_type=F32), give_dy, keep_dy, 2)
     give_x, keep_x = halves(rows_x)
-    gate_sum = replica_sum(lambda d: jnp.einsum("lcd,lcf->ldf", d, grad_gate, preferred_element_type=F32), give_x, keep_x, 1)
-    up_sum = replica_sum(lambda d: jnp.einsum("lcd,lcf->ldf", d, grad_up, preferred_element_type=F32), give_x, keep_x, 1)
+
+    def outer(rows, grads):
+        return jnp.einsum("lcd,lcf->ldf", rows, grads, preferred_element_type=F32)
+
+    if paired:
+        own_gate = outer(keep_x, grad_gate).astype(BF)
+        own_up = outer(keep_x, grad_up).astype(BF)
+        gate_sum = (own_gate.astype(F32) + outer(other_rows, other_gate).astype(BF).astype(F32)).astype(BF)
+        up_sum = (own_up.astype(F32) + outer(other_rows, other_up).astype(BF).astype(F32)).astype(BF)
+    else:
+        gate_sum = replica_sum(lambda d: outer(d, grad_gate), give_x, keep_x, 1)
+        up_sum = replica_sum(lambda d: outer(d, grad_up), give_x, keep_x, 1)
 
     row_grads = (
         jnp.einsum("lcf,ldf->lcd", grad_gate, gate_weight, preferred_element_type=F32)

time: 243 us -> 230 us (0.947)
  waiting for transfers between devices: 76.5 us -> 52 us
  matrix products: 54.1 us -> 60.1 us
  starting transfers between devices: 7.42 us -> 11 us
  local copies, waits for them, and re-layouts: 8.95 us -> 12.5 us
    ppermute x3 -> x5, waiting for transfers between devices: 70.9 us -> 52 us  [the longest x1 40.4 us: per_device(): other_pick = picks(lax.ppermute(mine, 'dp', SWAP), cap)]
    all_to_all x1, waiting for transfers between devices: 5.62 us -> 0.01 us  [per_device(): lax.all_to_all(back_route, 'expert', split_axis=0, concat_axis=0, tiled=T...]
    ppermute x3 -> x5, starting transfers between devices: 3.53 us -> 6.98 us  [the longest x1 2.94 us: per_device(): other_x = lax.ppermute(halves(tokens)[0], 'dp', SWAP)]
    unnamed x28 -> x24, local copies, waits for them, and re-layouts: 4.86 us -> 2.34 us
    dot_general x5 -> x7, matrix products: 19.4 us -> 20.5 us  [the longest x4 17.8 us: outer(): return jnp.einsum('lcd,lcf->ldf', rows, grads, preferred_element_type=F32)]
  transfers between devices with their start and end apart: 5 -> 8, of which waited for: 4 -> 2; matrix products, arithmetic and copies ran while one was open for 12% -> 29% of each run, Pallas kernels for 0% -> 33%
where the time goes in v4:
time: 230 us
  Pallas kernels  75.3 us (33%)
  matrix products  60.1 us (26%)
  waiting for transfers between devices  52 us (23%)
  between operations  14.3 us (6%)
  local copies, waits for them, and re-layouts  12.5 us (5%)
  starting transfers between devices  11 us (5%)
  other arithmetic  4.51 us (2%)
    pallas_call x1, Pallas kernels, gather(): pl.pallas_call(functools.partial(gather_kernel, chips, count), out_shape=...  75.3 us
    ppermute x1, waiting for transfers between devices, per_device(): other_pick = picks(lax.ppermute(mine, 'dp', SWAP), cap)  40.4 us
    dot_general x4, matrix products, outer(): return jnp.einsum('lcd,lcf->ldf', rows, grads, preferred_element_type=F32)  17.8 us
    ppermute x1, waiting for transfers between devices, per_device(): other_gate = lax.ppermute(grad_gate, 'dp', SWAP)  11.5 us
    dot_general x2, matrix products, per_device(): jnp.einsum('lcf,lcd->lfd', gated_hidden, d, preferred_element_type=F32)  8.55 us
    dot_general x1, matrix products, per_device(): jnp.einsum('lcd,ldf->lcf', rows_x, gate_weight, preferred_element_type=F32)  4.78 us
    dot_general x1, matrix products, per_device(): jnp.einsum('lcd,lfd->lcf', rows_dy, down_weight, preferred_element_type=F32)  4.67 us
  transfers between devices with their start and end apart: 8, of which 2 were waited for; matrix products, arithmetic and copies ran while one was open for 29% of the time, Pallas kernels for 33%

profile of v4, /device:TPU:0, one launch (start us, length us, event | category | flops | bytes accessed | tf_op | source)
XLA Modules:
  0.0 229.7 jit_solution(6404368498245039973)
XLA Ops:
  7.2 1.8 constant_dynamic-slice_fusion
  9.1 2.9 %collective-permute-start = (bf16[128,1024]{1,0:T(8,128)(2,1)}, bf16[128,1024]{1,0:T(8,128)(2,1)}, u32[]{:S(2)}, u32[]{:S(2)}) collective-permute-start(bf16[128,1024]{1,0:T(8,128)(2,1)} %constant_dynamic-slice_fusion), channel_id=1, source_target_pairs={{0,1},{1,0},{2,3},{3,2},{4,5},{5,4},{6,7},{7,6},{8,9},{9,8},{10,11... | collective-permute-start | bytes 786440 | tf_op jit(solution)/shard_map/ppermute | solution.py:155
  12.0 0.7 convert_element_type.119
  12.7 0.7 select_reduce_fusion.1
  13.5 0.6 pad.4.refs_2_
  14.1 75.3 %gather_line.1 = (bf16[8,128,2048]{2,1,0:T(8,128)(2,1)}, bf16[8,128,2048]{2,1,0:T(8,128)(2,1)}, bf16[8,128,128]{2,1,0:T(8,128)(2,1)}) custom-call(bf16[128,2048]{1,0:T(8,128)(2,1)} %refs_0_.1, bf16[128,2048]{1,0:T(8,128)(2,1)} %refs_1_.1, bf16[128,128]{1,0:T(8,128)(2,1)} %pad.4.refs_2_), custom_call_target="tpu_custom_call" | custom-call | bytes 17301504 | tf_op jit(solution)/shard_map/gather_line/pallas_call | solution.py:97
  89.4 1.8 broadcast_compare_fusion.1
  91.7 1.1 dynamic-slice_bitcast_fusion
  93.6 3.6 %convert_bitcast_fusion = bf16[2,8,72,2048]{3,2,0,1:T(8,128)(2,1)S(1)} fusion(bf16[8,128,2048]{2,1,0:T(8,128)(2,1)} %get-tuple-element.16, s32[2,8,128]{2,0,1:T(2,128)S(1)} %copy.46, pred[2,8,128]{2,0,1:T(4,128)(4,1)S(1)} %copy.47), kind=kOutput, calls=%fused_computation.4 | convolution fusion | flops 606633984 | bytes 8923136 | tf_op jit(solution)/shard_map/lsct,std->lscd/dot_general | solution.py:177
  97.2 2.5 %copy.49 = bf16[2,8,72,2048]{3,2,1,0:T(8,128)(2,1)} copy(bf16[2,8,72,2048]{3,2,0,1:T(8,128)(2,1)S(1)} %convert_bitcast_fusion) | data formatting | bytes 9437184 | tf_op jit(solution)/shard_map/convert_element_type | solution.py:177
  99.7 3.6 %convert_bitcast_fusion.1 = bf16[2,8,72,2048]{3,2,0,1:T(8,128)(2,1)S(1)} fusion(bf16[8,128,2048]{2,1,0:T(8,128)(2,1)} %get-tuple-element.15, s32[2,8,128]{2,0,1:T(2,128)S(1)} %copy.46, pred[2,8,128]{2,0,1:T(4,128)(4,1)S(1)} %copy.47), kind=kOutput, calls=%fused_computation.5 | convolution fusion | flops 606633984 | bytes 8923136 | tf_op jit(solution)/shard_map/lsct,std->lscd/dot_general | solution.py:169
  103.2 2.5 %copy.48 = bf16[2,8,72,2048]{3,2,1,0:T(8,128)(2,1)} copy(bf16[2,8,72,2048]{3,2,0,1:T(8,128)(2,1)S(1)} %convert_bitcast_fusion.1) | data formatting | bytes 9437184 | tf_op jit(solution)/shard_map/convert_element_type | solution.py:169
  106.1 4.8 %fusion.71 = f32[2,576,384]{2,1,0:T(8,128)S(1)} fusion(bf16[2,576,2048]{2,1,0:T(8,128)(2,1)} %bitcast.83, bf16[2,2048,384]{2,1,0:T(8,128)(2,1)S(1)} %copy-done), kind=kOutput, calls=%fused_computation.78 | convolution fusion | flops 1811939328 | bytes 9633792 | tf_op jit(solution)/shard_map/lcd,ldf->lcf/dot_general | solution.py:171
  110.9 2.6 %fusion.72 = f32[2,576,384]{2,1,0:T(8,128)S(1)} fusion(bf16[2,576,2048]{2,1,0:T(8,128)(2,1)S(1)} %bitcast.86, bf16[2,2048,384]{2,1,0:T(8,128)(2,1)S(1)} %copy-done.3), kind=kOutput, calls=%fused_computation.79 | convolution fusion | flops 1811939328 | bytes 9633792 | tf_op jit(solution)/shard_map/lcd,ldf->lcf/dot_general | solution.py:172
  113.5 4.7 %multiply_reduce_fusion = (bf16[2,576]{1,0:T(2,128)(2,1)S(1)}, bf16[2,576,384]{2,1,0:T(8,128)(2,1)}, bf16[2,576,384]{2,1,0:T(8,128)(2,1)}, bf16[2,576,384]{2,1,0:T(8,128)(2,1)}) fusion(f32[2,576,384]{2,1,0:T(8,128)S(1)} %fusion.72, f32[2,576,384]{2,1,0:T(8,128)S(1)} %fusion.71, f32[2,576]{1,0:T(2,128)S(1)} %mul.52, bf16[2,576,2048]{2,1,0:T(8,128)(2,1)S(1)} %bitcast.82, ...), kind=kOutput, calls=%fused_computation.22 | convolution fusion | flops 1820343168 | bytes 14064384 | tf_op jit(solution)/shard_map/lcd,lfd->lcf/dot_general | solution.py:179
  118.2 3.8 %fusion.73 = f32[2,576,2048]{2,1,0:T(8,128)S(1)} fusion(bf16[2,576,384]{2,1,0:T(8,128)(2,1)} %get-tuple-element.17, bf16[2,2048,384]{2,1,0:T(8,128)(2,1)S(1)} %copy-done), kind=kOutput, calls=%fused_computation.80 | convolution fusion | flops 1811939328 | bytes 13467648 | tf_op jit(solution)/shard_map/lcf,ldf->lcd/dot_general | solution.py:205
  122.1 4.1 %add_convert_fusion = bf16[2,576,2048]{2,1,0:T(8,128)(2,1)S(1)} fusion(f32[2,576,2048]{2,1,0:T(8,128)S(1)} %fusion.73, bf16[2,576,384]{2,1,0:T(8,128)(2,1)} %get-tuple-element.18, bf16[2,2048,384]{2,1,0:T(8,128)(2,1)S(1)} %copy-done.3), kind=kOutput, calls=%fused_computation | convolution fusion | flops 1816657920 | bytes 18186240 | tf_op jit(solution)/shard_map/lcf,ldf->lcd/dot_general | solution.py:206
  126.2 3.4 %bitcast_convert_fusion = bf16[8,128,2048]{2,1,0:T(8,128)(2,1)} fusion(bf16[2,8,72,2048]{3,2,1,0:T(8,128)(2,1)S(1)} %bitcast.77, s32[2,8,128]{2,0,1:T(2,128)S(1)} %copy.46, pred[2,8,128]{2,0,1:T(4,128)(4,1)S(1)} %copy.47), kind=kOutput, calls=%fused_computation.1 | convolution fusion | flops 606371840 | bytes 8923136 | tf_op jit(solution)/shard_map/lsct,lscd->std/dot_general | solution.py:208
  129.6 1.2 copy-done.9
  130.8 4.3 %fusion.30 = bf16[2,384,1024]{2,1,0:T(8,128)(2,1)} fusion(bf16[2,576,384]{2,1,0:T(8,128)(2,1)S(1)} %copy-done.9, bf16[2,576,2048]{2,1,0:T(8,128)(2,1)} %bitcast.78, s32[]{:T(128)S(6)} %select_n.29), kind=kOutput, calls=%fused_computation.31 | convolution fusion | flops 906756096 | bytes 4816900 | tf_op jit(solution)/shard_map/lcf,lcd->lfd/dot_general | solution.py:189
  135.6 1.5 collective-permute-start.1
  137.1 40.4 %collective-permute-done.1 = bf16[2,8,128]{0,2,1:T(8,128)(2,1)S(1)} collective-permute-done((bf16[2,8,128]{0,2,1:T(8,128)(2,1)S(1)}, bf16[2,8,128]{0,2,1:T(8,128)(2,1)S(1)}, u32[]{:S(2)}, u32[]{:S(2)}) %collective-permute-start.1) | collective-permute-done | bytes 4128 | tf_op jit(solution)/shard_map/ppermute | solution.py:162
  179.8 3.8 %all-to-all-start = ((bf16[8,2,128]{2,1,0:T(2,128)(2,1)}), bf16[8,2,128]{2,1,0:T(2,128)(2,1)S(1)}, u32[]{:S(2)}, u32[]{:S(2)}) async-start(bf16[8,2,128]{2,1,0:T(2,128)(2,1)} %convert_element_type.133), calls=%async_computation.1 | async-start | bytes 8192 | tf_op jit(solution)/shard_map/all_to_all | solution.py:214
  183.5 4.7 %fusion.24 = bf16[2,1024,384]{2,1,0:T(8,128)(2,1)} fusion(bf16[2,576,384]{2,1,0:T(8,128)(2,1)} %get-tuple-element.18, bf16[2,576,2048]{2,1,0:T(8,128)(2,1)} %bitcast.84, s32[]{:T(128)S(6)} %select_n.31), kind=kOutput, calls=%fused_computation.29 | convolution fusion | flops 906756096 | bytes 4816900 | tf_op jit(solution)/shard_map/lcd,lcf->ldf/dot_general | solution.py:193
  188.3 4.7 %fusion.21 = bf16[2,1024,384]{2,1,0:T(8,128)(2,1)} fusion(bf16[2,576,384]{2,1,0:T(8,128)(2,1)} %get-tuple-element.17, bf16[2,576,2048]{2,1,0:T(8,128)(2,1)} %bitcast.85, s32[]{:T(128)S(6)} %select_n.31), kind=kOutput, calls=%fused_computation.28 | convolution fusion | flops 906756096 | bytes 4816900 | tf_op jit(solution)/shard_map/lcd,lcf->ldf/dot_general | solution.py:193
  193.0 1.4 collective-permute-start.2
  195.1 4.2 %add_convert_fusion.1 = bf16[2,384,1024]{2,1,0:T(8,128)(2,1)} fusion(bf16[2,384,1024]{2,1,0:T(8,128)(2,1)S(1)} %collective-permute-done.4, bf16[2,576,384]{2,1,0:T(8,128)(2,1)S(1)} %copy-done.9, bf16[2,576,2048]{2,1,0:T(8,128)(2,1)} %bitcast.79, s32[]{:T(128)S(6)} %select_n.31), kind=kOutput, calls=%fused_computation.10 | convolution fusion | flops 909901824 | bytes 6389764 | tf_op jit(solution)/shard_map/lcf,lcd->lfd/dot_general | solution.py:189
  199.3 2.4 %convert_bitcast_fusion.2 = bf16[2,8,72,1024]{3,2,0,1:T(8,128)(2,1)S(1)} fusion(bf16[8,128,1024,1]{2,1,3,0:T(8,128)(2,1)} %bitcast.89, s32[2,8,128]{2,0,1:T(2,128)S(1)} %copy.53, pred[2,8,128]{2,0,1:T(4,128)(4,1)S(1)} %copy.54), kind=kOutput, calls=%fused_computation.17 | convolution fusion | flops 303464448 | bytes 4466688 | tf_op jit(solution)/shard_map/lsct,std->lscd/dot_general | solution.py:165
  202.0 1.1 copy-done.8
  203.1 4.2 %add_convert_fusion.2 = bf16[2,1024,384]{2,1,0:T(8,128)(2,1)} fusion(bf16[2,1024,384]{2,1,0:T(8,128)(2,1)S(1)} %copy-done.8, bf16[2,576,1024]{2,1,0:T(8,128)(2,1)S(1)} %bitcast.87, bf16[2,576,384]{2,1,0:T(8,128)(2,1)} %collective-permute-done.3), kind=kOutput, calls=%fused_computation.11 | convolution fusion | flops 909901824 | bytes 6389760 | tf_op jit(solution)/shard_map/lcd,lcf->ldf/dot_general | solution.py:193
  207.3 11.5 %collective-permute-done.2 = bf16[2,576,384]{2,1,0:T(8,128)(2,1)} collective-permute-done((bf16[2,576,384]{2,1,0:T(8,128)(2,1)}, bf16[2,576,384]{2,1,0:T(8,128)(2,1)}, u32[]{:S(2)}, u32[]{:S(2)}) %collective-permute-start.2) | collective-permute-done | bytes 884768 | tf_op jit(solution)/shard_map/ppermute | solution.py:186
  218.8 4.1 %add_convert_fusion.3 = bf16[2,1024,384]{2,1,0:T(8,128)(2,1)} fusion(bf16[2,1024,384]{2,1,0:T(8,128)(2,1)S(1)} %copy-done.7, bf16[2,576,1024]{2,1,0:T(8,128)(2,1)S(1)} %bitcast.88, bf16[2,576,384]{2,1,0:T(8,128)(2,1)} %collective-permute-done.2), kind=kOutput, calls=%fused_computation.12 | convolution fusion | flops 909901824 | bytes 6389760 | tf_op jit(solution)/shard_map/lcd,lcf->ldf/dot_general | solution.py:193
  (55 shorter events, 5.2 us)
Async XLA Ops:
  7.2 98.9 %copy-start = (bf16[2,2048,384]{2,1,0:T(8,128)(2,1)S(1)}, bf16[2,2048,384]{2,1,0:T(8,128)(2,1)}, u32[]{:S(2)}) copy-start(bf16[2,2048,384]{2,1,0:T(8,128)(2,1)} %param.11) | copy-start | bytes 9437188
  7.2 192.1 %all-gather.3.cloned.1.call-start = ((), (), s32[]{:S(2)}) async-start(), calls=%async_computation.3 | async-start | bytes 2359296 | tf_op jit(solution)/shard_map/all_gather | solution.py:164
  9.1 90.6 %collective-permute-start = (bf16[128,1024]{1,0:T(8,128)(2,1)}, bf16[128,1024]{1,0:T(8,128)(2,1)}, u32[]{:S(2)}, u32[]{:S(2)}) collective-permute-start(bf16[128,1024]{1,0:T(8,128)(2,1)} %constant_dynamic-slice_fusion), channel_id=1, source_target_pairs={{0,1},{1,0},{2,3},{3,2},{4,5},{5,4},{6,7},{7,6},{8,9},{9,8},{10,11... | collective-permute-start | bytes 786440 | tf_op jit(solution)/shard_map/ppermute | solution.py:155
  105.8 117.1 %reduce-scatter.2.cloned.1.call-start = ((), (), s32[]{:S(2)}) async-start(), calls=%async_computation.2 | async-start | bytes 4718592 | tf_op jit(solution)/shard_map/reduce_scatter | solution.py:209
  106.0 4.8 %copy-start.2 = (bf16[2,8,72,2048]{3,2,1,0:T(8,128)(2,1)S(1)}, bf16[2,8,72,2048]{3,2,1,0:T(8,128)(2,1)}, u32[]{:S(2)}) copy-start(bf16[2,8,72,2048]{3,2,1,0:T(8,128)(2,1)} %copy.48) | copy-start | bytes 14155780
  106.0 4.8 %copy-start.3 = (bf16[2,2048,384]{2,1,0:T(8,128)(2,1)S(1)}, bf16[2,2048,384]{2,1,0:T(8,128)(2,1)}, u32[]{:S(2)}) copy-start(bf16[2,2048,384]{2,1,0:T(8,128)(2,1)} %param.12) | copy-start | bytes 9437188
  106.0 7.5 %slice-start = ((s8[4718592]{0:T(1024)(128)(4,1)}), s8[4194304]{0:T(1024)(128)(4,1)S(1)}, s32[]{:S(2)}) async-start(s8[4718592]{0:T(1024)(128)(4,1)} %bitcast.80), calls=%async_computation.4 | async-start | bytes 8388608
  110.9 2.7 %slice-start.1 = ((s8[4718592]{0:T(1024)(128)(4,1)}), s8[524288]{0:T(1024)(128)(4,1)S(1)}, s32[]{:S(2)}) async-start(s8[4718592]{0:T(1024)(128)(4,1)} %bitcast.80), calls=%async_computation.5 | async-start | bytes 1048576
  110.9 2.7 %copy-start.6 = (bf16[2,384,2048]{2,1,0:T(8,128)(2,1)S(1)}, bf16[2,384,2048]{2,1,0:T(8,128)(2,1)}, u32[]{:S(2)}) copy-start(bf16[2,384,2048]{2,1,0:T(8,128)(2,1)} %param.13) | copy-start | bytes 9437188
  129.6 1.2 copy-start.9
  130.8 4.8 %copy-start.4 = (bf16[2,8,128]{0,2,1:T(8,128)(2,1)S(1)}, bf16[2,8,128]{0,2,1:T(8,128)(2,1)}, u32[]{:S(2)}) copy-start(bf16[2,8,128]{0,2,1:T(8,128)(2,1)} %get-tuple-element.22) | copy-start | bytes 12292
  135.1 60.0 %collective-permute-start.4 = (bf16[2,384,1024]{2,1,0:T(8,128)(2,1)}, bf16[2,384,1024]{2,1,0:T(8,128)(2,1)S(1)}, u32[]{:S(2)}, u32[]{:S(2)}) collective-permute-start(bf16[2,384,1024]{2,1,0:T(8,128)(2,1)} %fusion.30), channel_id=1, source_target_pairs={{0,1},{1,0},{2,3},{3,2},{4,5},{5,4},{6,7},{7,6},{8,9},{9,8},{10,11... | collective-permute-start | bytes 4718600 | tf_op jit(solution)/shard_map/ppermute | solution.py:135
  135.6 42.0 %collective-permute-start.1 = (bf16[2,8,128]{0,2,1:T(8,128)(2,1)S(1)}, bf16[2,8,128]{0,2,1:T(8,128)(2,1)S(1)}, u32[]{:S(2)}, u32[]{:S(2)}) collective-permute-start(bf16[2,8,128]{0,2,1:T(8,128)(2,1)S(1)} %copy-done.4), channel_id=1, source_target_pairs={{0,1},{1,0},{2,3},{3,2},{4,5},{5,4},{6,7},{7,6},{8,9},{9,8},{10,11... | collective-permute-start | bytes 12296 | tf_op jit(solution)/shard_map/ppermute | solution.py:162
  178.3 23.7 %collective-permute-start.3 = (bf16[2,576,384]{2,1,0:T(8,128)(2,1)}, bf16[2,576,384]{2,1,0:T(8,128)(2,1)}, u32[]{:S(2)}, u32[]{:S(2)}) collective-permute-start(bf16[2,576,384]{2,1,0:T(8,128)(2,1)} %get-tuple-element.18), channel_id=1, source_target_pairs={{0,1},{1,0},{2,3},{3,2},{4,5},{5,4},{6,7},{7,6},{8,9},{9,8},{10,11... | collective-permute-start | bytes 2654216 | tf_op jit(solution)/shard_map/ppermute | solution.py:187
  179.8 14.7 %all-to-all-start = ((bf16[8,2,128]{2,1,0:T(2,128)(2,1)}), bf16[8,2,128]{2,1,0:T(2,128)(2,1)S(1)}, u32[]{:S(2)}, u32[]{:S(2)}) async-start(bf16[8,2,128]{2,1,0:T(2,128)(2,1)} %convert_element_type.133), calls=%async_computation.1 | async-start | bytes 8192 | tf_op jit(solution)/shard_map/all_to_all | solution.py:214
  188.2 6.2 %copy-start.5 = (s32[128,8]{0,1:T(8,128)S(1)}, s32[128,8]{0,1:T(8,128)}, u32[]{:S(2)}) copy-start(s32[128,8]{0,1:T(8,128)} %param.9) | copy-start | bytes 12292
  193.0 25.8 %collective-permute-start.2 = (bf16[2,576,384]{2,1,0:T(8,128)(2,1)}, bf16[2,576,384]{2,1,0:T(8,128)(2,1)}, u32[]{:S(2)}, u32[]{:S(2)}) collective-permute-start(bf16[2,576,384]{2,1,0:T(8,128)(2,1)} %get-tuple-element.17), channel_id=1, source_target_pairs={{0,1},{1,0},{2,3},{3,2},{4,5},{5,4},{6,7},{7,6},{8,9},{9,8},{10,11... | collective-permute-start | bytes 2654216 | tf_op jit(solution)/shard_map/ppermute | solution.py:186
  201.7 1.4 copy-start.8
  203.1 15.7 %copy-start.7 = (bf16[2,1024,384]{2,1,0:T(8,128)(2,1)S(1)}, bf16[2,1024,384]{2,1,0:T(8,128)(2,1)}, u32[]{:S(2)}) copy-start(bf16[2,1024,384]{2,1,0:T(8,128)(2,1)} %fusion.21) | copy-start | bytes 4718596
  203.1 19.8 %copy-start.1 = (bf16[2,2048,384]{2,1,0:T(8,128)(2,1)S(1)}, bf16[2,2048,384]{2,1,0:T(8,128)(2,1)}, u32[]{:S(2)}) copy-start(bf16[2,2048,384]{2,1,0:T(8,128)(2,1)} %param.11) | copy-start | bytes 9437188
Sparse Core Ops, SparseCore 0:
  105.9 28.2 all-gather.2
  137.1 49.4 reduce-scatter.1
